TPU v7x, 32 devices: a whole 2x2x4 slice. The times are simulated.
32 devices in a mesh: tok: 4 (over z), head: 8 (over y, x, core).
Axes of the slice: x: 2, y: 2, z: 4, core: 2. Of those that a mesh axis runs over, the one named last changes fastest.
Arguments:
- stream: bfloat16 [1024, 7168], P('tok'), may hold values from -400 to 400
- row_tree_nodes: int32 [1024], replicated, may hold values from 0 to 1023, as said below
- input_norm_gain: bfloat16 [7168], replicated, may hold values from 0.099609375 to 1.8984375
- query_key_value_weight: bfloat16 [7168, 3, 7168], P('head', None, 'tok'), may hold values from -0.141736677 to 0.141736677
- adapter_down_weight: bfloat16 [7168, 128], replicated, may hold values from -0.0625 to 0.0625
- adapter_up_weight: bfloat16 [128, 3, 7168], P('head', None, 'tok'), may hold values from -0.23925781 to 0.23925781
- key_value_cache: bfloat16 [2, 16, 2048, 7168], P(None, 'head', None, 'tok'), may hold values from -104 to 104
- cache_length: int32 [16], P('head'), may hold values from 256 to 2048, as said below
- parents: int32 [16, 64], P('head'), may hold values from 0 to 62, as said below
- accepted: int32 [16, 8], P('head'), may hold values from 0 to 63, as said below
- output_weight: bfloat16 [7168, 3584], P('tok', 'head'), may hold values from -0.375 to 0.375
Outputs:
- attended: bfloat16 [1024, 3584], P('tok', 'head')
- accepted_kv: bfloat16 [2, 16, 8, 7168], P(None, 'head', None, 'tok')
Inputs may be any that keep to these rules, and one draw needn't show every extreme that they name: row_tree_nodes is a permutation of the 1024 node numbers; every aligned block of 128 rows holds exactly 8 nodes of every request. `cache_length`: at least one request's cache holds exactly 2048 positions. parents[r, 0] = 0 marks the root; parents[r, n] < n for n > 0. `accepted`: each row lists 8 nodes of its request's tree, each the parent of the next.
All inputs are finite; a program needn't handle non-finite values.
Results may differ from a plain program's by a relative error of at most 0.014.
Values may be sent and summed in bfloat16 or wider, within the bound.
No kernel may reach another device: no remote copies, remote signals or barrier semaphores. Data moves between devices by JAX's collectives and lax.ppermute only.
A program may use at most 192 MiB of HBM per device.

v0:
```python
import jax
import jax.numpy as jnp
from jax import lax
from jax.sharding import PartitionSpec as P

HEAD_SIZE = 224
NODES = 64


def ancestors_of(parents):
    parent_links = jax.nn.one_hot(parents, NODES, dtype=jnp.float32)
    identity_matrix = jnp.eye(NODES, dtype=jnp.float32)
    ancestry = jnp.minimum(identity_matrix[None] + parent_links, 1.0)
    for squaring in range(NODES.bit_length()):
        ancestry = jnp.minimum(
            jnp.einsum("rnm,rmk->rnk", ancestry, ancestry, precision=lax.Precision.HIGHEST), 1.0
        )
    return ancestry


def on_device(
    stream,
    row_tree_nodes,
    input_norm_gain,
    query_key_value_weight,
    adapter_down_weight,
    adapter_up_weight,
    key_value_cache,
    cache_length,
    parents,
    accepted,
    output_weight,
):
    owner_index = lax.axis_index("head")
    feature_rows = query_key_value_weight.shape[0]
    device_width = query_key_value_weight.shape[2]
    adapter_rank_rows = adapter_up_weight.shape[0]
    local_heads = device_width // HEAD_SIZE
    request_count = key_value_cache.shape[1]
    cache_span = key_value_cache.shape[2]
    wide_rows = stream.astype(jnp.float32)
    inverse_rms = lax.rsqrt(jnp.mean(wide_rows * wide_rows, axis=1, keepdims=True) + 1e-05)
    normalized_input = (wide_rows * inverse_rms * input_norm_gain.astype(jnp.float32)).astype(
        jnp.bfloat16
    )
    reduced_rank_rows = jnp.dot(
        normalized_input, adapter_down_weight, preferred_element_type=jnp.float32
    ).astype(jnp.bfloat16)
    feature_block = lax.dynamic_slice_in_dim(
        normalized_input, owner_index * feature_rows, feature_rows, 1
    )
    rank_block = lax.dynamic_slice_in_dim(
        reduced_rank_rows, owner_index * adapter_rank_rows, adapter_rank_rows, 1
    )
    gathered_features, gathered_ranks = (
        lax.all_gather(feature_block, "tok", axis=0, tiled=True),
        lax.all_gather(rank_block, "tok", axis=0, tiled=True),
    )
    projection = query_key_value_weight.reshape(feature_rows, 3 * device_width)
    lifting_matrix = adapter_up_weight.reshape(adapter_rank_rows, 3 * device_width)
    node_to_row = jnp.argsort(row_tree_nodes)
    part_sum = jnp.dot(
        gathered_features[node_to_row], projection, preferred_element_type=jnp.float32
    )
    node_rows = lax.psum_scatter(
        part_sum
        + jnp.dot(gathered_ranks[node_to_row], lifting_matrix, preferred_element_type=jnp.float32),
        "head",
        scatter_dimension=0,
        tiled=True,
    ).astype(jnp.bfloat16)
    triple = node_rows.reshape(request_count, NODES, 3, local_heads, HEAD_SIZE)
    queries = triple[:, :, 0]
    tree_key_rows = triple[:, :, 1]
    tree_value_rows = triple[:, :, 2]
    ancestry = ancestors_of(parents)
    attention_score_scale = HEAD_SIZE ** (-0.5)
    tree_score_matrix = (
        jnp.einsum("rnhd,rmhd->rhnm", queries, tree_key_rows, preferred_element_type=jnp.float32)
        * attention_score_scale
    )
    tree_score_matrix = jnp.where(ancestry[:, None] > 0.5, tree_score_matrix, -jnp.inf)
    keys_cache = key_value_cache[0].reshape(request_count, cache_span, local_heads, HEAD_SIZE)
    values_cache = key_value_cache[1].reshape(request_count, cache_span, local_heads, HEAD_SIZE)
    scores = (
        jnp.einsum("rnhd,rchd->rhnc", queries, keys_cache, preferred_element_type=jnp.float32)
        * attention_score_scale
    )
    positions = lax.broadcasted_iota(jnp.int32, (1, 1, 1, cache_span), 3)
    scores = jnp.where(positions < cache_length[:, None, None, None], scores, -jnp.inf)
    tree_top = jnp.max(tree_score_matrix, axis=-1, keepdims=True)
    largest = jnp.maximum(tree_top, jnp.max(scores, axis=-1, keepdims=True))
    cache_exp = jnp.exp(scores - largest)
    tree_exp = jnp.exp(tree_score_matrix - largest)
    totals = jnp.sum(cache_exp, axis=-1, keepdims=True) + jnp.sum(tree_exp, axis=-1, keepdims=True)
    cache_weights = (cache_exp / totals).astype(jnp.bfloat16)
    tree_weight_matrix = (tree_exp / totals).astype(jnp.bfloat16)
    attention = jnp.einsum(
        "rhnc,rchd->rnhd", cache_weights, values_cache, preferred_element_type=jnp.float32
    )
    attention = attention + jnp.einsum(
        "rhnm,rmhd->rnhd", tree_weight_matrix, tree_value_rows, preferred_element_type=jnp.float32
    )
    head_rows = attention.astype(jnp.bfloat16).reshape(request_count * NODES, device_width)
    node_table = node_rows.reshape(request_count, NODES, 3, device_width)
    chosen = jnp.take_along_axis(node_table, accepted[:, :, None, None], axis=1)
    accepted_kv = jnp.stack([chosen[:, :, 1], chosen[:, :, 2]])
    everything = lax.all_gather(head_rows, "head", axis=0, tiled=True)
    attended = lax.psum_scatter(
        jnp.dot(
            everything[row_tree_nodes], output_weight, preferred_element_type=jnp.float32
        ).astype(jnp.bfloat16),
        "tok",
        scatter_dimension=0,
        tiled=True,
    )
    return (attended, accepted_kv)


def solution(mesh):
    placed = (
        P("tok", None),
        P(),
        P(),
        P("head", None, "tok"),
        P(),
        P("head", None, "tok"),
        P(None, "head", None, "tok"),
        P("head"),
        P("head", None),
        P("head", None),
        P("tok", "head"),
    )
    return jax.shard_map(
        on_device,
        mesh=mesh,
        in_specs=placed,
        out_specs=(P("tok", "head"), P(None, "head", None, "tok")),
        check_vma=False,
    )
```

profile of v0, /device:TPU:0, one launch (start us, length us, event | category | flops | bytes accessed | tf_op | source)
XLA Modules:
  0.0 358.6 jit_solution(1213190858059930061)
XLA Ops:
  7.2 3.0 fusion.1
  10.3 0.7 convert_element_type.39
  11.0 3.1 fusion.3
  14.1 1.8 copy-done.3
  15.8 0.8 constant_dynamic-slice_fusion
  16.8 13.4 %copy.21 = bf16[896,3,1792]{0,2,1:T(8,128)(2,1)} copy(bf16[896,3,1792]{2,0,1:T(8,128)(2,1)} %param.14) | data formatting | bytes 19267584 | tf_op args[3]
  30.2 4.4 %sort.17 = (s32[1024]{0:T(1024)}, s32[1024]{0:T(1024)S(1)}) sort(s32[1024]{0:T(1024)S(1)} %copy-done.5, s32[1024]{0:T(1024)S(1)} %iota.34), dimensions={0}, to_apply=%region_1.0 | sort | flops 10240 | bytes 16384 | tf_op jit(solution)/shard_map/jit(argsort)/sort | solution.py:61
  34.5 3.2 fusion.31
  37.8 18.2 %all_gather.10 = bf16[1024,16]{1,0:T(8,128)(2,1)S(1)} all-gather(bf16[256,16]{1,0:T(8,128)(2,1)S(1)} %dynamic-slice_convert_fusion), channel_id=1, replica_groups=mesh['tok'=4,'head'=8] {'tok'}, dimensions={0}, use_global_device_ids=true | all-gather | bytes 40960 | tf_op jit(solution)/shard_map/all_gather | solution.py:57
  56.0 3.2 gather_fusion.1
  59.2 8.9 %fusion.32 = f32[1024,5376]{1,0:T(8,128)} fusion(bf16[1024,16]{1,0:T(8,128)(2,1)S(1)} %gather_fusion.1, bf16[16,5376]{1,0:T(8,128)(2,1)S(1)} %bitcast.66), kind=kOutput, calls=%fused_computation.72 | convolution fusion | flops 176160768 | bytes 22224896 | tf_op jit(solution)/shard_map/dot_general | solution.py:67
  68.1 6.4 %gather_fusion = bf16[1024,896]{1,0:T(8,128)(2,1)S(1)} fusion(bf16[1024,896]{1,0:T(8,128)(2,1)} %all-gather.3.cloned.1.call-done, s32[1024]{0:T(1024)S(1)} %fusion.23), kind=kCustom, calls=%fused_computation | custom fusion | bytes 3674112 | tf_op jit(solution)/shard_map/gather | solution.py:63
  74.5 22.8 %convolution_add_fusion = f32[1024,5376]{1,0:T(8,128)} fusion(f32[1024,5376]{1,0:T(8,128)} %fusion.32, bf16[1024,896]{1,0:T(8,128)(2,1)S(1)} %gather_fusion, bf16[896,5376]{0,1:T(8,128)(2,1)} %bitcast.64), kind=kOutput, calls=%fused_computation.4 | convolution fusion | flops 9870508032 | bytes 55508992 | tf_op jit(solution)/shard_map/dot_general | solution.py:62
  99.6 25.5 %fusion.28 = (bf16[1,2,2048,1792]{3,2,1,0:T(8,128)(2,1)}, bf16[1,2,2048,1792]{3,2,1,0:T(8,128)(2,1)}) fusion(bf16[2,2,2048,1792]{3,2,1,0:T(8,128)(2,1)} %param.17), kind=kLoop, calls=%fused_computation.68 | loop fusion | bytes 58720256 | tf_op jit(solution)/shard_map/slice | solution.py:84
  125.1 19.9 %copy.27 = bf16[1,2,2048,1792]{2,3,1,0:T(8,128)(2,1)} copy(bf16[1,2,2048,1792]{3,2,1,0:T(8,128)(2,1)} %get-tuple-element.4) | data formatting | bytes 29360128 | tf_op jit(solution)/shard_map/slice | solution.py:84
  145.1 19.7 %copy.24 = bf16[1,2,2048,1792]{2,3,1,0:T(8,128)(2,1)} copy(bf16[1,2,2048,1792]{3,2,1,0:T(8,128)(2,1)} %get-tuple-element.5) | data formatting | bytes 29360128 | tf_op jit(solution)/shard_map/slice | solution.py:83
  164.8 74.4 %reduce-scatter.3.cloned.1.call-done = f32[128,5376]{1,0:T(8,128)} async-done(((f32[1024,5376]{1,0:T(8,128)}), f32[128,5376]{1,0:T(8,128)}) %reduce-scatter.3.cloned.1.call-update) | async-done | bytes 2752528 | tf_op jit(solution)/shard_map/reduce_scatter | solution.py:65
  239.3 1.9 convert_element_type.42
  241.2 2.5 reshape.94
  244.1 8.1 %fusion = (f32[2,8,64]{2,1,0:T(8,128)S(1)}, f32[2,8,64,2048]{3,2,1,0:T(8,128)S(1)}) fusion(pred[2,2048]{1,0:T(4,128)(4,1)S(1)} %iota_compare_fusion.3, bf16[2,2048,8,224]{1,3,2,0:T(8,128)(2,1)} %bitcast.62, bf16[2,64,1,8,224]{4,3,2,1,0:T(8,128)(2,1)S(1)} %get-tuple-element.6), kind=kOutput, calls=%fused_computation.10 | convolution fusion | flops 945814528 | bytes 23535616 | tf_op jit(solution)/shard_map/rnhd,rchd->rhnc/dot_general | solution.py:86
  252.4 3.1 copy-done.2
  255.5 1.9 fusion.4
  257.4 1.4 convolution_bitcast_fusion
  258.8 15.5 %fusion.9 = bf16[2,64,8,224]{3,1,2,0:T(8,128)(2,1)S(1)} fusion(f32[2,64,8,224]{3,1,2,0:T(8,128)} %convolution_bitcast_fusion, bf16[2,2048,8,224]{1,3,2,0:T(8,128)(2,1)} %bitcast.63, f32[2,8,64,2048]{3,2,1,0:T(8,128)} %copy-done.2, f32[2,8,64]{2,1,0:T(8,128)S(1)} %add.63, f32[2,8,64]{2,1,0:T(8,128)S(1)} %max.8, pred[2,2048]{1,0:T(4,128)(4,1)S(1)} %iota_compare_fusion.3), kind=kOutput, calls=%fused_computation.21 | convolution fusion | flops 950468608 | bytes 24457216 | tf_op jit(solution)/shard_map/rhnc,rchd->rnhd/dot_general | solution.py:98
  274.6 1.4 reshape.95
  276.1 34.6 %all-gather.5.cloned.1.call-done = bf16[1024,1792]{1,0:T(8,128)(2,1)} async-done(((bf16[128,1792]{1,0:T(8,128)(2,1)}), bf16[1024,1792]{1,0:T(8,128)(2,1)}) %all-gather.5.cloned.1.call-update) | async-done | bytes 3670032 | tf_op jit(solution)/shard_map/all_gather | solution.py:108
  310.7 10.8 %gather_fusion.2 = bf16[1024,1792]{1,0:T(8,128)(2,1)} fusion(bf16[1024,1792]{1,0:T(8,128)(2,1)} %all-gather.5.cloned.1.call-done, s32[1024]{0:T(1024)S(1)} %fusion.24), kind=kCustom, calls=%fused_computation.2 | custom fusion | bytes 7344128 | tf_op jit(solution)/shard_map/gather | solution.py:111
  321.5 5.3 %convolution_convert_fusion = bf16[1024,448]{0,1:T(8,128)(2,1)} fusion(bf16[1024,1792]{1,0:T(8,128)(2,1)} %gather_fusion.2, bf16[1792,448]{0,1:T(8,128)(2,1)} %param.21), kind=kOutput, calls=%fused_computation.17 | convolution fusion | flops 1644625920 | bytes 6193152 | tf_op jit(solution)/shard_map/dot_general | solution.py:110
  327.0 2.0 reshape.96
  329.0 2.3 gather_fusion.3
  331.4 0.7 pad_maximum_fusion
  332.0 20.1 %reduce-scatter.5.cloned.1.call-done = bf16[256,448]{0,1:T(8,128)(2,1)} async-done(((bf16[1024,448]{0,1:T(8,128)(2,1)}), bf16[256,448]{0,1:T(8,128)(2,1)}) %reduce-scatter.5.cloned.1.call-update) | async-done | bytes 229392 | tf_op jit(solution)/shard_map/reduce_scatter | solution.py:109
  (52 shorter events, 3.6 us)
Async XLA Ops:
  7.2 27.4 %copy-start = (bf16[7168,128]{1,0:T(8,128)(2,1)S(1)}, bf16[7168,128]{1,0:T(8,128)(2,1)}, u32[]{:S(2)}) copy-start(bf16[7168,128]{1,0:T(8,128)(2,1)} %param.15) | copy-start | bytes 5505028
  7.2 9.6 %copy-start.4 = (bf16[16,3,1792]{2,0,1:T(8,128)(2,1)S(1)}, bf16[16,3,1792]{2,0,1:T(8,128)(2,1)}, u32[]{:S(2)}) copy-start(bf16[16,3,1792]{2,0,1:T(8,128)(2,1)} %param.16) | copy-start | bytes 516100
  7.2 60.9 %all-gather.3.cloned.1.call-start = ((), (), s32[]{:S(2)}) async-start(), calls=%async_computation.2 | async-start | bytes 2293760 | tf_op jit(solution)/shard_map/all_gather | solution.py:56
  14.0 1.8 copy-start.3
  16.7 222.6 %reduce-scatter.3.cloned.1.call-start = ((), (), s32[]{:S(2)}) async-start(), calls=%async_computation.3 | async-start | bytes 24772608 | tf_op jit(solution)/shard_map/reduce_scatter | solution.py:65
  16.8 13.4 %copy-start.5 = (s32[1024]{0:T(1024)S(1)}, s32[1024]{0:T(1024)}, u32[]{:S(2)}) copy-start(s32[1024]{0:T(1024)} %param.12) | copy-start | bytes 12292
  97.3 0.7 copy-start.6
  97.4 213.3 %all-gather.5.cloned.1.call-start = ((), (), s32[]{:S(2)}) async-start(), calls=%async_computation.4 | async-start | bytes 4128768 | tf_op jit(solution)/shard_map/all_gather | solution.py:108
  145.1 19.7 %copy-start.8 = (s32[2]{0:T(128)S(1)}, s32[2]{0:T(128)}, u32[]{:S(2)}) copy-start(s32[2]{0:T(128)} %param.18) | copy-start | bytes 28
  252.3 3.2 copy-start.2
  276.0 76.1 %reduce-scatter.5.cloned.1.call-start = ((), (), s32[]{:S(2)}) async-start(), calls=%async_computation.5 | async-start | bytes 1146880 | tf_op jit(solution)/shard_map/reduce_scatter | solution.py:109
  310.7 41.4 %copy-start.1 = (bf16[7168,128]{1,0:T(8,128)(2,1)S(1)}, bf16[7168,128]{1,0:T(8,128)(2,1)}, u32[]{:S(2)}) copy-start(bf16[7168,128]{1,0:T(8,128)(2,1)} %param.15) | copy-start | bytes 5505028
  321.5 5.3 %copy-start.7 = (s32[2,8]{1,0:T(2,128)S(1)}, s32[2,8]{1,0:T(2,128)}, u32[]{:S(2)}) copy-start(s32[2,8]{1,0:T(2,128)} %param.20) | copy-start | bytes 196
Sparse Core Ops, SparseCore 0:
  16.8 48.2 all-gather.2
  97.5 141.7 reduce-scatter.2
  276.2 34.4 all-gather.4
  327.0 25.0 reduce-scatter.4
where the time goes:
time: 360 us; the launch traced here: 359 us
  waiting for transfers between devices  129 us (36%)
  local copies, waits for them, and re-layouts  114 us (32%)
  matrix products  67 us (19%)
  blocking collectives  18.2 us (5%)
  other arithmetic  15.9 us (4%)
  between operations  14 us (4%)
    reduce_scatter x1, waiting for transfers between devices, on_device(): lax.psum_scatter(part_sum + jnp.dot(gathered_ranks[node_to_row], lifting_...  74.4 us
    slice x2, local copies, waits for them, and re-layouts, on_device(): key_value_cache[1]  45.5 us
    all_gather x1, waiting for transfers between devices, on_device(): everything = lax.all_gather(head_rows, 'head', axis=0, tiled=True)  34.6 us
    dot_general x1, matrix products, on_device(): jnp.dot(gathered_features[node_to_row], projection, preferred_element_typ...  22.8 us
    reduce_scatter x1, waiting for transfers between devices, on_device(): lax.psum_scatter(jnp.dot(everything[row_tree_nodes], output_weight, prefe...  20.1 us
    slice x1, local copies, waits for them, and re-layouts, on_device(): key_value_cache[0]  19.7 us
    unnamed x19, local copies, waits for them, and re-layouts  18.9 us
    all_gather x1, blocking collectives, on_device(): lax.all_gather(rank_block, 'tok', axis=0, tiled=True)  18.2 us
  transfers between devices with their start and end apart: 4, of which 3 were waited for; matrix products, arithmetic and copies ran while one was open for 29% of the time, Pallas kernels for 0%

commit v1 on v0

--- a/solution.py
+++ b/solution.py
@@ -1,10 +1,398 @@
+import functools
+
 import jax
 import jax.numpy as jnp
 from jax import lax
+from jax.experimental import pallas as pl
+from jax.experimental.pallas import tpu as pltpu
 from jax.sharding import PartitionSpec as P
 
 HEAD_SIZE = 224
 NODES = 64
+LANES = 128
+F32 = jnp.float32
+BF16 = jnp.bfloat16
+VMEM_BYTES = 50 * 2**20
+
+
+def dot(a, b, dims=((1,), (0,))):
+    return lax.dot_general(a, b, (dims, ((), ())), preferred_element_type=F32)
+
+
+def whole(shape):
+    return pl.BlockSpec(shape, lambda *_: (0,) * len(shape))
+
+
+def params():
+    return pltpu.CompilerParams(vmem_limit_bytes=VMEM_BYTES)
+
+
+def row_to_column(row):
+    size = row.shape[1]
+    eye = lax.broadcasted_iota(jnp.int32, (size, size), 0) == lax.broadcasted_iota(
+        jnp.int32, (size, size), 1
+    )
+    return jnp.sum(jnp.where(eye, row, 0), axis=1, keepdims=True)
+
+
+def rank_in_plane(row):
+    before = row_to_column(row) < row
+    return jnp.sum(before.astype(jnp.int32), axis=0, keepdims=True)
+
+
+def norm_kernel(slots, rank_rows, ids_ref, stream_ref, gain_ref, down_ref, first_ref, second_ref,
+                place_ref, normed):
+    me = lax.axis_index("head")
+    plane = lax.axis_index("tok")
+    rows, width = stream_ref.shape
+    step = 32
+    gain = gain_ref[...].astype(F32)
+
+    def chunk(i, carry):
+        at = pl.ds(pl.multiple_of(i * step, step), step)
+        wide = stream_ref[at, :].astype(F32)
+        rstd = lax.rsqrt(jnp.sum(wide * wide, axis=1, keepdims=True) / width + 1e-05)
+        normed[at, :] = (wide * rstd * gain).astype(BF16)
+        return carry
+
+    lax.fori_loop(0, rows // step, chunk, 0)
+    low = dot(normed[...], down_ref[...]).astype(BF16)
+    ranks = low.shape[1]
+    pick = lax.broadcasted_iota(jnp.int32, (ranks, LANES), 0) == (
+        lax.broadcasted_iota(jnp.int32, (ranks, LANES), 1) + me * rank_rows
+    )
+    pick &= lax.broadcasted_iota(jnp.int32, (ranks, LANES), 1) < rank_rows
+    low = dot(low, pick.astype(BF16)).astype(BF16)
+    ids = ids_ref[pl.ds(plane, 1), :]
+    rank = rank_in_plane(ids)
+    owner = ids // (2 * NODES)
+    second = (ids // NODES) % 2
+    apart = owner ^ me
+    even = (owner & 1) == 0
+    bit_x = (apart >> 1) & 1
+    bit_y = (apart >> 2) & 1
+    order = (apart & 1) * 4 + jnp.where(even, bit_x * 2 + bit_y, bit_y * 2 + bit_x)
+    position = second * (rows // 2) + order * slots + rank % slots
+    place = (lax.broadcasted_iota(jnp.int32, (rows, rows), 0) == position).astype(BF16)
+    place_ref[...] = place
+    columns = first_ref.shape[1] - LANES
+    block = normed[:, pl.ds(pl.multiple_of(me * columns, LANES), columns)]
+    sorted_block = dot(place, block).astype(BF16)
+    sorted_low = dot(place, low).astype(BF16)
+    half = rows // 2
+    first_ref[:, :columns] = sorted_block[:half]
+    second_ref[:, :columns] = sorted_block[half:]
+    first_ref[:, columns:] = sorted_low[:half]
+    second_ref[:, columns:] = sorted_low[half:]
+
+
+def prep_kernel(slots, ids_ref, parents_ref, accepted_ref, mask_ref, chosen_ref):
+    me = lax.axis_index("head")
+    plane = lax.axis_index("tok")
+    planes, rows = ids_ref.shape
+    for j in range(2):
+        nodes = []
+        for k in range(planes):
+            ids = ids_ref[pl.ds(plane ^ k, 1), :]
+            rank = rank_in_plane(ids)
+            spot = lax.broadcasted_iota(jnp.int32, (slots, rows), 0) + (me * 2 + j) * slots
+            nodes.append(
+                jnp.sum(jnp.where(rank == spot, ids, 0), axis=1, keepdims=True)
+                - (me * 2 + j) * NODES
+            )
+        nodes = jnp.concatenate(nodes, axis=0)
+        lanes = lax.broadcasted_iota(jnp.int32, (NODES, NODES), 1)
+        rows_of = lax.broadcasted_iota(jnp.int32, (NODES, NODES), 0)
+        named = (nodes == lanes).astype(BF16)
+        parent = row_to_column(parents_ref[j : j + 1, :])
+        reach = ((parent == lanes) | (rows_of == lanes)).astype(BF16)
+        for _ in range((NODES - 1).bit_length()):
+            reach = jnp.minimum(dot(reach, reach), 1.0).astype(BF16)
+        mask_ref[j] = dot(dot(named, reach).astype(BF16), named, ((1,), (1,)))
+        accepted = row_to_column(accepted_ref[j : j + 1, :])
+        depth = accepted.shape[0]
+        wanted = (accepted == lax.broadcasted_iota(jnp.int32, (depth, NODES), 1)).astype(BF16)
+        chosen_ref[j] = dot(wanted, named, ((1,), (1,)))
+
+
+def project_kernel(pieces, groups, rank_rows, *refs):
+    lhs_refs = refs[:pieces]
+    weight_ref, up_ref, keep_ref, send_ref = refs[pieces:]
+    columns = weight_ref.shape[0]
+    at = 0
+    for lhs_ref in lhs_refs:
+        rows = lhs_ref.shape[0] // groups
+        for g in range(groups):
+            lhs = lhs_ref[g * rows : (g + 1) * rows, :]
+            total = dot(lhs[:, :columns], weight_ref[...])
+            total += dot(lhs[:, columns : columns + rank_rows], up_ref[...])
+            keep_ref[at : at + rows // 2, :] = total[: rows // 2]
+            send_ref[at : at + rows // 2, :] = total[rows // 2 :].astype(BF16)
+            at += rows // 2
+
+
+def project(pieces, groups, weight, up):
+    parts, columns, width = weight.shape
+    rank_rows = up.shape[1]
+    tile = width // 2
+    rows = sum(piece.shape[0] for piece in pieces) // 2
+    return pl.pallas_call(
+        functools.partial(project_kernel, len(pieces), groups, rank_rows),
+        grid=(parts, 2),
+        in_specs=[whole(piece.shape) for piece in pieces]
+        + [
+            pl.BlockSpec((None, columns, tile), lambda p, c: (p, 0, c)),
+            pl.BlockSpec((None, rank_rows, tile), lambda p, c: (p, 0, c)),
+        ],
+        out_specs=[
+            pl.BlockSpec((rows, tile), lambda p, c: (0, p * 2 + c)),
+            pl.BlockSpec((rows, tile), lambda p, c: (0, p * 2 + c)),
+        ],
+        out_shape=[
+            jax.ShapeDtypeStruct((rows, parts * width), F32),
+            jax.ShapeDtypeStruct((rows, parts * width), BF16),
+        ],
+        compiler_params=params(),
+        cost_estimate=pl.CostEstimate(
+            flops=4 * rows * (columns + 128) * parts * width,
+            bytes_accessed=2 * columns * parts * width + 6 * rows * parts * width,
+            transcendentals=0,
+        ),
+    )(*pieces, weight, up)
+
+
+def attend_kernel(span, heads, length_ref, query_ref, key_ref, value_ref, mask_ref, chosen_ref,
+                  cache_key_ref, cache_value_ref, out_ref, kept_ref, spread, top, total, acc):
+    block = pl.program_id(1)
+    width = query_ref.shape[1]
+    scale = HEAD_SIZE ** (-0.5)
+    head_of_lane = lax.broadcasted_iota(jnp.int32, (1, width), 1) // HEAD_SIZE
+    length = length_ref[0]
+
+    def fold(scores, values, first):
+        peak = jnp.max(scores, axis=1, keepdims=True)
+        if not first:
+            before = top[...]
+            peak = jnp.maximum(before, peak)
+        weights = jnp.exp(scores - peak)
+        gained = jnp.sum(weights, axis=1, keepdims=True)
+        part = dot(weights.astype(BF16), values)
+        if first:
+            total[...] = gained
+            acc[...] = part
+        else:
+            shrink = jnp.exp(before - peak)
+            total[...] = total[...] * shrink + gained
+            acc[...] = acc[...] * shrink + part
+        top[...] = peak
+
+    @pl.when(block == 0)
+    def start():
+        query = query_ref[...]
+        for h in range(heads):
+            spread[h * NODES : (h + 1) * NODES, :] = jnp.where(head_of_lane == h, query, 0)
+        scores = dot(spread[...], key_ref[...], ((1,), (1,))) * scale
+        allowed = jnp.concatenate([mask_ref[...]] * heads, axis=0) > 0.5
+        fold(jnp.where(allowed, scores, -1e30), value_ref[...], True)
+        pick = chosen_ref[...].astype(BF16)
+        kept_ref[0] = dot(pick, key_ref[...]).astype(BF16)
+        kept_ref[1] = dot(pick, value_ref[...]).astype(BF16)
+
+    @pl.when(block * span < length)
+    def cached():
+        scores = dot(spread[...], cache_key_ref[...], ((1,), (1,))) * scale
+        spot = lax.broadcasted_iota(jnp.int32, (1, span), 1) + block * span
+        fold(jnp.where(spot < length, scores, -1e30), cache_value_ref[...], False)
+
+    @pl.when(block == pl.num_programs(1) - 1)
+    def finish():
+        share = acc[...] / total[...]
+        out = jnp.zeros((NODES, width), F32)
+        for h in range(heads):
+            out = jnp.where(head_of_lane == h, share[h * NODES : (h + 1) * NODES, :], out)
+        out_ref[...] = out.astype(BF16)
+
+
+def attend(j, lengths, triple, masks, chosen, cache):
+    cache_span, width = cache.shape[2:]
+    tile = 4 * HEAD_SIZE
+    groups = width // tile
+    span = min(1024, cache_span)
+    depth = chosen.shape[1]
+
+    def cached(part):
+        def index(g, b, length):
+            return (part, j, jnp.minimum(b, (length[0] - 1) // span), g)
+
+        return pl.BlockSpec((None, None, span, tile), index)
+
+    def column(part):
+        return pl.BlockSpec((NODES, tile), lambda g, b, length: (0, part * groups + g))
+
+    return pl.pallas_call(
+        functools.partial(attend_kernel, span, 4),
+        grid_spec=pltpu.PrefetchScalarGridSpec(
+            num_scalar_prefetch=1,
+            grid=(groups, cache_span // span),
+            in_specs=[
+                column(0),
+                column(1),
+                column(2),
+                pl.BlockSpec((None, NODES, NODES), lambda g, b, length: (j, 0, 0)),
+                pl.BlockSpec((None, depth, NODES), lambda g, b, length: (j, 0, 0)),
+                cached(0),
+                cached(1),
+            ],
+            out_specs=[
+                pl.BlockSpec((NODES, tile), lambda g, b, length: (0, g)),
+                pl.BlockSpec((2, depth, tile), lambda g, b, length: (0, 0, g)),
+            ],
+            scratch_shapes=[
+                pltpu.VMEM((4 * NODES, tile), BF16),
+                pltpu.VMEM((4 * NODES, 1), F32),
+                pltpu.VMEM((4 * NODES, 1), F32),
+                pltpu.VMEM((4 * NODES, tile), F32),
+            ],
+        ),
+        out_shape=[
+            jax.ShapeDtypeStruct((NODES, width), BF16),
+            jax.ShapeDtypeStruct((2, depth, width), BF16),
+        ],
+        compiler_params=params(),
+        cost_estimate=pl.CostEstimate(
+            flops=16 * NODES * cache_span * width,
+            bytes_accessed=4 * cache_span * width,
+            transcendentals=NODES * cache_span * 4 * groups,
+        ),
+    )(lengths[j : j + 1], triple, triple, triple, masks, chosen, cache, cache)
+
+
+def lift_kernel(rows_ref, weight_ref, out_ref):
+    rows = rows_ref[...].reshape(-1, rows_ref.shape[-1])
+    out_ref[...] = dot(weight_ref[...], rows, ((1,), (1,)))
+
+
+def lift(rows, weight):
+    owners, planes, slots, width = rows.shape
+    wide = weight.shape[0]
+    return pl.pallas_call(
+        lift_kernel,
+        grid=(planes,),
+        in_specs=[
+            pl.BlockSpec((owners, None, slots, width), lambda k: (0, k, 0, 0)),
+            whole(weight.shape),
+        ],
+        out_specs=pl.BlockSpec((None, wide, owners * slots), lambda k: (k, 0, 0)),
+        out_shape=jax.ShapeDtypeStruct((planes, wide, owners * slots), F32),
+        compiler_params=params(),
+        cost_estimate=pl.CostEstimate(
+            flops=2 * owners * planes * slots * width * wide,
+            bytes_accessed=2 * rows.size + 2 * weight.size,
+            transcendentals=0,
+        ),
+    )(rows, weight)
+
+
+def final_kernel(pieces, place_ref, *refs):
+    own = refs[:2]
+    others = refs[2:-1]
+    out_ref = refs[-1]
+    sums = []
+    for j in range(2):
+        total = own[j][...]
+        for piece in others[j * pieces : (j + 1) * pieces]:
+            total = total + piece[...].astype(F32)
+        sums.append(total.astype(BF16))
+    out_ref[...] = dot(jnp.concatenate(sums, axis=1), place_ref[...]).astype(BF16)
+
+
+def on_device(
+    stream,
+    row_tree_nodes,
+    input_norm_gain,
+    query_key_value_weight,
+    adapter_down_weight,
+    adapter_up_weight,
+    key_value_cache,
+    cache_length,
+    parents,
+    accepted,
+    output_weight,
+):
+    rows, width_in = stream.shape
+    planes = row_tree_nodes.shape[0] // rows
+    owners = width_in // query_key_value_weight.shape[0]
+    slots = rows // (2 * owners)
+    columns = query_key_value_weight.shape[0]
+    width = query_key_value_weight.shape[2]
+    rank_rows = adapter_up_weight.shape[0]
+    weight = jnp.swapaxes(query_key_value_weight, 0, 1)
+    up = jnp.swapaxes(adapter_up_weight, 0, 1)
+    down = jnp.swapaxes(output_weight, 0, 1)
+    ids = row_tree_nodes.reshape(planes, rows)
+
+    def first_mask(h):
+        return 2 if h % 2 == 0 else 4
+
+    core_pairs = [(h, h ^ 1) for h in range(owners)]
+    first_pairs = [(h, h ^ first_mask(h)) for h in range(owners)]
+    second_pairs = [(h, h ^ (6 - first_mask(h))) for h in range(owners)]
+
+    def across(array, k):
+        return lax.ppermute(array, "tok", [(z, z ^ k) for z in range(planes)])
+
+    feature = jax.ShapeDtypeStruct((rows // 2, columns + LANES), BF16)
+    first, second, place = pl.pallas_call(
+        functools.partial(norm_kernel, slots, rank_rows),
+        out_shape=[feature, feature, jax.ShapeDtypeStruct((rows, rows), BF16)],
+        scratch_shapes=[pltpu.VMEM((rows, width_in), BF16)],
+        compiler_params=params(),
+    )(ids, stream, input_norm_gain.reshape(1, -1), adapter_down_weight)
+    near = [first, second]
+    far = [[across(near[j], k) for k in range(1, planes)] for j in range(2)]
+    depth = accepted.shape[1]
+    masks, chosen = pl.pallas_call(
+        functools.partial(prep_kernel, slots),
+        out_shape=[
+            jax.ShapeDtypeStruct((2, NODES, NODES), F32),
+            jax.ShapeDtypeStruct((2, depth, NODES), F32),
+        ],
+        compiler_params=params(),
+    )(ids, parents, accepted)
+
+    def scatter(keep, send, batch):
+        keep = keep.reshape(batch, 4 * slots, -1)
+        send = send.reshape(batch, 4 * slots, -1)
+        for pairs, left in ((core_pairs, 4), (first_pairs, 2), (second_pairs, 1)):
+            got = lax.ppermute(send, "head", pairs)
+            added = keep + got.astype(F32)
+            if left == 1:
+                return added.astype(BF16)
+            cut = left * slots // 2
+            send = added[:, cut:].astype(BF16)
+            keep = added[:, :cut]
+
+    own = scatter(*project(near, 1, weight, up), 2)
+    finished = []
+    kept = []
+    for j in range(2):
+        rest = scatter(*project(far[j], 1, weight, up), planes - 1)
+        triple = jnp.concatenate([own[j], rest.reshape(-1, rest.shape[-1])], axis=0)
+        gathered, saved = attend(j, cache_length, triple, masks, chosen, key_value_cache)
+        kept.append(saved)
+        gathered = gathered.reshape(1, planes, slots, width)
+        for pairs in (second_pairs, first_pairs, core_pairs):
+            gathered = jnp.concatenate([gathered, lax.ppermute(gathered, "head", pairs)], axis=0)
+        lifted = lift(gathered, down)
+        finished.append(
+            (lifted[0], [across(lifted[k].astype(BF16), k) for k in range(1, planes)])
+        )
+    attended = pl.pallas_call(
+        functools.partial(final_kernel, planes - 1),
+        out_shape=jax.ShapeDtypeStruct((output_weight.shape[1], rows), BF16),
+        compiler_params=params(),
+    )(place, finished[0][0], finished[1][0], *finished[0][1], *finished[1][1])
+    return jnp.swapaxes(attended, 0, 1), jnp.stack(kept, axis=1)
 
 
 def ancestors_of(parents):
@@ -18,7 +406,7 @@
     return ancestry
 
 
-def on_device(
+def plain_on_device(
     stream,
     row_tree_nodes,
     input_norm_gain,
@@ -131,8 +519,9 @@
         P("head", None),
         P("tok", "head"),
     )
+    sized = mesh.shape["head"] == 8 and mesh.shape["tok"] == 4
     return jax.shard_map(
-        on_device,
+        on_device if sized else plain_on_device,
         mesh=mesh,
         in_specs=placed,
         out_specs=(P("tok", "head"), P(None, "head", None, "tok")),

time: 360 us -> 206 us (0.57)
  local copies, waits for them, and re-layouts: 114 us -> 5.17 us
  Pallas kernels: 0 us -> 70.7 us
  matrix products: 67 us -> 0 us
  waiting for transfers between devices: 129 us -> 81.4 us
  starting transfers between devices: 0.16 us -> 40.3 us
  blocking collectives: 18.2 us -> 0 us
  between operations: 14 us -> 0.95 us
  other arithmetic: 15.9 us -> 6.95 us
    reduce_scatter x2 -> x0, waiting for transfers between devices: 94.5 us -> none  [the longest x1 74.4 us: on_device(): lax.psum_scatter(part_sum + jnp.dot(gathered_ranks[node_to_row], lifting_...]
    ppermute x0 -> x27, waiting for transfers between devices: none -> 81.4 us  [the longest x9 33.9 us: scatter(): got = lax.ppermute(send, 'head', pairs)]
    pallas_call x0 -> x10, Pallas kernels: none -> 70.7 us  [the longest x3 30.4 us: project(): pl.pallas_call(functools.partial(project_kernel, len(pieces), groups, ran...]
    dot_general x15 -> x0, matrix products: 67 us -> none  [the longest x1 22.8 us: on_device(): jnp.dot(gathered_features[node_to_row], projection, preferred_element_typ...]
    slice x4 -> x7, local copies, waits for them, and re-layouts: 65.2 us -> 1.02 us  [the longest x1 0.6 us: attend(): lengths[j:j + 1]]
    ppermute x0 -> x27, starting transfers between devices: none -> 40.3 us  [the longest x12 27.9 us: across(): return lax.ppermute(array, 'tok', [(z, z ^ k) for z in range(planes)])]
    all_gather x2 -> x0, waiting for transfers between devices: 34.6 us -> none  [the longest x1 34.6 us: on_device(): everything = lax.all_gather(head_rows, 'head', axis=0, tiled=True)]
    gather x5 -> x0, local copies, waits for them, and re-layouts: 22.7 us -> none  [the longest x1 10.8 us: on_device(): everything[row_tree_nodes]]
  transfers between devices with their start and end apart: 4 -> 27, of which waited for: 3 -> 12; matrix products, arithmetic and copies ran while one was open for 29% -> 3% of each run, Pallas kernels for 0% -> 19%
where the time goes in v1:
time: 206 us; the launch traced here: 205 us
  waiting for transfers between devices  81.4 us (40%)
  Pallas kernels  70.7 us (34%)
  starting transfers between devices  40.3 us (20%)
  other arithmetic  6.95 us (3%)
  local copies, waits for them, and re-layouts  5.17 us (3%)
    ppermute x9, waiting for transfers between devices, scatter(): got = lax.ppermute(send, 'head', pairs)  33.9 us
    ppermute x12, waiting for transfers between devices, across(): return lax.ppermute(array, 'tok', [(z, z ^ k) for z in range(planes)])  31.4 us
    pallas_call x3, Pallas kernels, project(): pl.pallas_call(functools.partial(project_kernel, len(pieces), groups, ran...  30.4 us
    ppermute x12, starting transfers between devices, across(): return lax.ppermute(array, 'tok', [(z, z ^ k) for z in range(planes)])  27.9 us
    pallas_call x2, Pallas kernels, attend(): pl.pallas_call(functools.partial(attend_kernel, span, 4), grid_spec=pltpu...  23.6 us
    ppermute x6, waiting for transfers between devices, on_device(): lax.ppermute(gathered, 'head', pairs)  16 us
    ppermute x9, starting transfers between devices, scatter(): got = lax.ppermute(send, 'head', pairs)  9.84 us
    pallas_call x2, Pallas kernels, lift(): pl.pallas_call(lift_kernel, grid=(planes,), in_specs=[pl.BlockSpec((owner...  7.68 us
  transfers between devices with their start and end apart: 27, of which 12 were waited for; matrix products, arithmetic and copies ran while one was open for 3% of the time, Pallas kernels for 19%

profile of v1, /device:TPU:0, one launch (start us, length us, event | category | flops | bytes accessed | tf_op | source)
XLA Modules:
  0.0 205.5 jit_solution(4165263988005779318)
XLA Ops:
  3.6 6.0 %shard_map.122 = (bf16[128,1024]{1,0:T(8,128)(2,1)S(1)}, bf16[128,1024]{1,0:T(8,128)(2,1)S(1)}, bf16[256,256]{1,0:T(8,128)(2,1)S(1)}) custom-call(s32[4,256]{1,0:T(4,128)S(1)} %reshape.46.ids_ref, bf16[256,7168]{1,0:T(8,128)(2,1)} %stream_ref.1, bf16[1,7168]{1,0:T(2,128)(2,1)S(1)} %reshape.47.gain_ref, bf16[7168,128]{1,0:T(8,128)(2,1)S(1)} %copy-done.1), custom_call_target="tpu_custom_call" | custom-call | tf_op jit(solution)/shard_map/pallas_call | solution.py:345
  9.6 9.0 %shard_map.123 = (f32[128,5376]{1,0:T(8,128)}, bf16[128,5376]{1,0:T(8,128)(2,1)S(1)}) custom-call(bf16[128,1024]{1,0:T(8,128)(2,1)S(1)} %get-tuple-element.18.refs_0_, bf16[128,1024]{1,0:T(8,128)(2,1)S(1)} %get-tuple-element.19.refs_1_, bf16[3,896,1792]{2,1,0:T(8,128)(2,1)} %bitcast.60, bf16[3,16,1792]{2,1,0:T(8,128)(2,1)S(1)} %bitcast.51), custom_call_target="tpu_custom_call" | custom-call | flops 2818572288 | bytes 13762560 | tf_op jit(solution)/shard_map/pallas_call | solution.py:139
  19.1 2.6 %collective-permute-start.3 = (bf16[128,1024]{1,0:T(8,128)(2,1)S(1)}, bf16[128,1024]{1,0:T(8,128)(2,1)S(1)}, u32[]{:S(2)}, u32[]{:S(2)}) collective-permute-start(bf16[128,1024]{1,0:T(8,128)(2,1)S(1)} %get-tuple-element.18.refs_0_), channel_id=1, source_target_pairs={{0,8},{8,0},{16,24},{24,16},{1,9},{9,1},{17,25},{25,17},{2,10},{10... | collective-permute-start | bytes 786440 | tf_op jit(solution)/shard_map/ppermute | solution.py:342
  21.7 2.6 %collective-permute-start.4 = (bf16[128,1024]{1,0:T(8,128)(2,1)S(1)}, bf16[128,1024]{1,0:T(8,128)(2,1)S(1)}, u32[]{:S(2)}, u32[]{:S(2)}) collective-permute-start(bf16[128,1024]{1,0:T(8,128)(2,1)S(1)} %get-tuple-element.18.refs_0_), channel_id=1, source_target_pairs={{0,16},{8,24},{16,0},{24,8},{1,17},{9,25},{17,1},{25,9},{2,18},{10... | collective-permute-start | bytes 786440 | tf_op jit(solution)/shard_map/ppermute | solution.py:342
  25.2 3.5 %collective-permute-start.13 = (bf16[128,1024]{1,0:T(8,128)(2,1)S(1)}, bf16[128,1024]{1,0:T(8,128)(2,1)S(1)}, u32[]{:S(2)}, u32[]{:S(2)}) collective-permute-start(bf16[128,1024]{1,0:T(8,128)(2,1)S(1)} %get-tuple-element.19.refs_1_), channel_id=1, source_target_pairs={{0,16},{8,24},{16,0},{24,8},{1,17},{9,25},{17,1},{25,9},{2,18},{10... | collective-permute-start | bytes 786440 | tf_op jit(solution)/shard_map/ppermute | solution.py:342
  28.6 2.0 convert_add_fusion.2
  30.8 3.3 %collective-permute-done.3.refs_0_ = bf16[128,1024]{1,0:T(8,128)(2,1)S(1)} collective-permute-done((bf16[128,1024]{1,0:T(8,128)(2,1)S(1)}, bf16[128,1024]{1,0:T(8,128)(2,1)S(1)}, u32[]{:S(2)}, u32[]{:S(2)}) %collective-permute-start.3) | collective-permute-done | bytes 262176 | tf_op jit(solution)/shard_map/ppermute | solution.py:342
  34.0 3.1 %collective-permute-start.14 = (bf16[128,1024]{1,0:T(8,128)(2,1)S(1)}, bf16[128,1024]{1,0:T(8,128)(2,1)S(1)}, u32[]{:S(2)}, u32[]{:S(2)}) collective-permute-start(bf16[128,1024]{1,0:T(8,128)(2,1)S(1)} %get-tuple-element.19.refs_1_), channel_id=1, source_target_pairs={{0,24},{8,16},{16,8},{24,0},{1,25},{9,17},{17,9},{25,1},{2,26},{10... | collective-permute-start | bytes 786440 | tf_op jit(solution)/shard_map/ppermute | solution.py:342
  37.2 5.9 %collective-permute-done.4.refs_1_ = bf16[128,1024]{1,0:T(8,128)(2,1)S(1)} collective-permute-done((bf16[128,1024]{1,0:T(8,128)(2,1)S(1)}, bf16[128,1024]{1,0:T(8,128)(2,1)S(1)}, u32[]{:S(2)}, u32[]{:S(2)}) %collective-permute-start.4) | collective-permute-done | bytes 262176 | tf_op jit(solution)/shard_map/ppermute | solution.py:342
  44.5 10.7 %shard_map.124 = (f32[192,5376]{1,0:T(8,128)}, bf16[192,5376]{1,0:T(8,128)(2,1)S(1)}) custom-call(bf16[128,1024]{1,0:T(8,128)(2,1)S(1)} %collective-permute-done.3.refs_0_, bf16[128,1024]{1,0:T(8,128)(2,1)S(1)} %collective-permute-done.4.refs_1_, bf16[128,1024]{1,0:T(8,128)(2,1)S(1)} %collective-permute-done.5.refs_2_, bf16[3,896,1792]{2,1,0:T(8,128)(2,1)} %bitcast.61, ...), custom_call_target="tpu_custom_call" | custom-call | flops 4227858432 | bytes 15826944 | tf_op jit(solution)/shard_map/pallas_call | solution.py:139
  55.2 2.0 shard_map.125
  57.8 7.7 %collective-permute-done.13.refs_1_ = bf16[128,1024]{1,0:T(8,128)(2,1)S(1)} collective-permute-done((bf16[128,1024]{1,0:T(8,128)(2,1)S(1)}, bf16[128,1024]{1,0:T(8,128)(2,1)S(1)}, u32[]{:S(2)}, u32[]{:S(2)}) %collective-permute-start.13) | collective-permute-done | bytes 262176 | tf_op jit(solution)/shard_map/ppermute | solution.py:342
  65.5 10.7 %shard_map.128 = (f32[192,5376]{1,0:T(8,128)}, bf16[192,5376]{1,0:T(8,128)(2,1)S(1)}) custom-call(bf16[128,1024]{1,0:T(8,128)(2,1)S(1)} %collective-permute-done.12.refs_0_, bf16[128,1024]{1,0:T(8,128)(2,1)S(1)} %collective-permute-done.13.refs_1_, bf16[128,1024]{1,0:T(8,128)(2,1)S(1)} %collective-permute-done.14.refs_2_, bf16[3,896,1792]{2,1,0:T(8,128)(2,1)} %bitcast.62, ...), custom_call_target="tpu_custom_call" | custom-call | flops 4227858432 | bytes 15826944 | tf_op jit(solution)/shard_map/pallas_call | solution.py:139
  76.4 1.6 collective-permute-start.2
  79.0 1.5 collective-permute-start.7
  82.6 3.4 %collective-permute-done.2 = bf16[2,16,5376]{2,1,0:T(8,128)(2,1)S(1)} collective-permute-done((bf16[2,16,5376]{2,1,0:T(8,128)(2,1)S(1)}, bf16[2,16,5376]{2,1,0:T(8,128)(2,1)S(1)}, u32[]{:S(2)}, u32[]{:S(2)}) %collective-permute-start.2) | collective-permute-done | bytes 344096 | tf_op jit(solution)/shard_map/ppermute | solution.py:367
  86.1 8.2 %collective-permute-done.7 = bf16[3,32,5376]{2,1,0:T(8,128)(2,1)S(1)} collective-permute-done((bf16[3,32,5376]{2,1,0:T(8,128)(2,1)S(1)}, bf16[3,32,5376]{2,1,0:T(8,128)(2,1)S(1)}, u32[]{:S(2)}, u32[]{:S(2)}) %collective-permute-start.7) | collective-permute-done | bytes 1032224 | tf_op jit(solution)/shard_map/ppermute | solution.py:367
  94.6 1.6 collective-permute-start.8
  96.2 14.8 %collective-permute-done.16 = bf16[3,32,5376]{2,1,0:T(8,128)(2,1)S(1)} collective-permute-done((bf16[3,32,5376]{2,1,0:T(8,128)(2,1)S(1)}, bf16[3,32,5376]{2,1,0:T(8,128)(2,1)S(1)}, u32[]{:S(2)}, u32[]{:S(2)}) %collective-permute-start.16) | collective-permute-done | bytes 1032224 | tf_op jit(solution)/shard_map/ppermute | solution.py:367
  111.1 1.6 collective-permute-start.17
  112.8 7.5 %collective-permute-done.17 = bf16[3,16,5376]{2,1,0:T(8,128)(2,1)S(1)} collective-permute-done((bf16[3,16,5376]{2,1,0:T(8,128)(2,1)S(1)}, bf16[3,16,5376]{2,1,0:T(8,128)(2,1)S(1)}, u32[]{:S(2)}, u32[]{:S(2)}) %collective-permute-start.17) | collective-permute-done | bytes 516128 | tf_op jit(solution)/shard_map/ppermute | solution.py:367
  120.5 11.7 %shard_map.126 = (bf16[64,1792]{1,0:T(8,128)(2,1)S(1)}, bf16[2,8,1792]{2,1,0:T(8,128)(2,1)S(1)}) custom-call(s32[1]{0:T(128)} %get-tuple-element.43.length_ref, bf16[64,5376]{1,0:T(8,128)(2,1)S(1)} %get-tuple-element.44.query_ref.key_ref.value_ref, bf16[64,5376]{1,0:T(8,128)(2,1)S(1)} %get-tuple-element.44.query_ref.key_ref.value_ref, ...), custom_call_target="tpu_custom_call" | custom-call | flops 3758096384 | bytes 14680064 | tf_op jit(solution)/shard_map/pallas_call | solution.py:232
  132.3 1.6 collective-permute-start.9
  133.8 11.9 %shard_map.129 = (bf16[64,1792]{1,0:T(8,128)(2,1)S(1)}, bf16[2,8,1792]{2,1,0:T(8,128)(2,1)S(1)}) custom-call(s32[1]{0:T(128)} %get-tuple-element.42.length_ref, bf16[64,5376]{1,0:T(8,128)(2,1)S(1)} %get-tuple-element.45.query_ref.key_ref.value_ref, bf16[64,5376]{1,0:T(8,128)(2,1)S(1)} %get-tuple-element.45.query_ref.key_ref.value_ref, ...), custom_call_target="tpu_custom_call" | custom-call | flops 3758096384 | bytes 14680064 | tf_op jit(solution)/shard_map/pallas_call | solution.py:232
  146.4 7.9 %collective-permute-done.18 = bf16[1,4,16,1792]{3,2,1,0:T(8,128)(2,1)S(1)} collective-permute-done((bf16[1,4,16,1792]{3,2,1,0:T(8,128)(2,1)S(1)}, bf16[1,4,16,1792]{3,2,1,0:T(8,128)(2,1)S(1)}, u32[]{:S(2)}, u32[]{:S(2)}) %collective-permute-start.18) | collective-permute-done | bytes 229408 | tf_op jit(solution)/shard_map/ppermute | solution.py:385
  155.2 7.7 %collective-permute-done.19 = bf16[2,4,16,1792]{3,2,1,0:T(8,128)(2,1)S(1)} collective-permute-done((bf16[2,4,16,1792]{3,2,1,0:T(8,128)(2,1)S(1)}, bf16[2,4,16,1792]{3,2,1,0:T(8,128)(2,1)S(1)}, u32[]{:S(2)}, u32[]{:S(2)}) %collective-permute-start.19) | collective-permute-done | bytes 458784 | tf_op jit(solution)/shard_map/ppermute | solution.py:385
  165.3 3.8 %shard_map.127 = f32[4,448,128]{2,1,0:T(8,128)S(1)} custom-call(bf16[8,4,16,1792]{3,2,1,0:T(8,128)(2,1)} %pad_maximum_fusion.rows_ref, bf16[448,1792]{1,0:T(8,128)(2,1)S(1)} %bitcast.36), custom_call_target="tpu_custom_call" | custom-call | flops 822083584 | bytes 3440640 | tf_op jit(solution)/shard_map/pallas_call | solution.py:278
  170.7 3.8 %shard_map.130 = f32[4,448,128]{2,1,0:T(8,128)S(1)} custom-call(bf16[8,4,16,1792]{3,2,1,0:T(8,128)(2,1)} %pad_maximum_fusion.1.rows_ref, bf16[448,1792]{1,0:T(8,128)(2,1)S(1)} %bitcast.37), custom_call_target="tpu_custom_call" | custom-call | flops 822083584 | bytes 3440640 | tf_op jit(solution)/shard_map/pallas_call | solution.py:278
  174.6 8.3 %collective-permute-start.21 = (bf16[448,128]{1,0:T(8,128)(2,1)S(1)}, bf16[448,128]{1,0:T(8,128)(2,1)S(1)}, u32[]{:S(2)}, u32[]{:S(2)}) collective-permute-start(bf16[448,128]{1,0:T(8,128)(2,1)S(1)} %get-tuple-element.39), channel_id=1, source_target_pairs={{0,8},{8,0},{16,24},{24,16},{1,9},{9,1},{17,25},{25,17},{2,10},{10... | collective-permute-start | bytes 344072 | tf_op jit(solution)/shard_map/ppermute | solution.py:342
  186.5 2.0 collective-permute-start.25
  189.9 4.8 %collective-permute-done.22.refs_3_ = bf16[448,128]{1,0:T(8,128)(2,1)S(1)} collective-permute-done((bf16[448,128]{1,0:T(8,128)(2,1)S(1)}, bf16[448,128]{1,0:T(8,128)(2,1)S(1)}, u32[]{:S(2)}, u32[]{:S(2)}) %collective-permute-start.22) | collective-permute-done | bytes 114720 | tf_op jit(solution)/shard_map/ppermute | solution.py:342
  194.7 9.8 %collective-permute-done.25.refs_6_ = bf16[448,128]{1,0:T(8,128)(2,1)S(1)} collective-permute-done((bf16[448,128]{1,0:T(8,128)(2,1)S(1)}, bf16[448,128]{1,0:T(8,128)(2,1)S(1)}, u32[]{:S(2)}, u32[]{:S(2)}) %collective-permute-start.25) | collective-permute-done | bytes 114720 | tf_op jit(solution)/shard_map/ppermute | solution.py:342
  (82 shorter events, 21.9 us)
Async XLA Ops:
  3.6 6.1 %copy-start.4 = (bf16[16,3,1792]{2,0,1:T(8,128)(2,1)S(1)}, bf16[16,3,1792]{2,0,1:T(8,128)(2,1)}, u32[]{:S(2)}) copy-start(bf16[16,3,1792]{2,0,1:T(8,128)(2,1)} %param.16) | copy-start | bytes 516100
  18.6 6.5 %collective-permute-start = (bf16[2,64,5376]{2,1,0:T(8,128)(2,1)S(1)}, bf16[2,64,5376]{2,1,0:T(8,128)(2,1)S(1)}, u32[]{:S(2)}, u32[]{:S(2)}) collective-permute-start(bf16[2,64,5376]{2,1,0:T(8,128)(2,1)S(1)} %bitcast.50), channel_id=1, source_target_pairs={{0,1},{1,0},{2,3},{3,2},{4,5},{5,4},{6,7},{7,6},{8,9},{9,8},{10,11... | collective-permute-start | bytes 4128776 | tf_op jit(solution)/shard_map/ppermute | solution.py:367
  19.1 14.9 %collective-permute-start.3 = (bf16[128,1024]{1,0:T(8,128)(2,1)S(1)}, bf16[128,1024]{1,0:T(8,128)(2,1)S(1)}, u32[]{:S(2)}, u32[]{:S(2)}) collective-permute-start(bf16[128,1024]{1,0:T(8,128)(2,1)S(1)} %get-tuple-element.18.refs_0_), channel_id=1, source_target_pairs={{0,8},{8,0},{16,24},{24,16},{1,9},{9,1},{17,25},{25,17},{2,10},{10... | collective-permute-start | bytes 786440 | tf_op jit(solution)/shard_map/ppermute | solution.py:342
  21.7 21.4 %collective-permute-start.4 = (bf16[128,1024]{1,0:T(8,128)(2,1)S(1)}, bf16[128,1024]{1,0:T(8,128)(2,1)S(1)}, u32[]{:S(2)}, u32[]{:S(2)}) collective-permute-start(bf16[128,1024]{1,0:T(8,128)(2,1)S(1)} %get-tuple-element.18.refs_0_), channel_id=1, source_target_pairs={{0,16},{8,24},{16,0},{24,8},{1,17},{9,25},{17,1},{25,9},{2,18},{10... | collective-permute-start | bytes 786440 | tf_op jit(solution)/shard_map/ppermute | solution.py:342
  24.3 20.3 %collective-permute-start.5 = (bf16[128,1024]{1,0:T(8,128)(2,1)S(1)}, bf16[128,1024]{1,0:T(8,128)(2,1)S(1)}, u32[]{:S(2)}, u32[]{:S(2)}) collective-permute-start(bf16[128,1024]{1,0:T(8,128)(2,1)S(1)} %get-tuple-element.18.refs_0_), channel_id=1, source_target_pairs={{0,24},{8,16},{16,8},{24,0},{1,25},{9,17},{17,9},{25,1},{2,26},{10... | collective-permute-start | bytes 786440 | tf_op jit(solution)/shard_map/ppermute | solution.py:342
  24.3 33.6 %collective-permute-start.12 = (bf16[128,1024]{1,0:T(8,128)(2,1)S(1)}, bf16[128,1024]{1,0:T(8,128)(2,1)S(1)}, u32[]{:S(2)}, u32[]{:S(2)}) collective-permute-start(bf16[128,1024]{1,0:T(8,128)(2,1)S(1)} %get-tuple-element.19.refs_1_), channel_id=1, source_target_pairs={{0,8},{8,0},{16,24},{24,16},{1,9},{9,1},{17,25},{25,17},{2,10},{10... | collective-permute-start | bytes 786440 | tf_op jit(solution)/shard_map/ppermute | solution.py:342
  25.2 40.3 %collective-permute-start.13 = (bf16[128,1024]{1,0:T(8,128)(2,1)S(1)}, bf16[128,1024]{1,0:T(8,128)(2,1)S(1)}, u32[]{:S(2)}, u32[]{:S(2)}) collective-permute-start(bf16[128,1024]{1,0:T(8,128)(2,1)S(1)} %get-tuple-element.19.refs_1_), channel_id=1, source_target_pairs={{0,16},{8,24},{16,0},{24,8},{1,17},{9,25},{17,1},{25,9},{2,18},{10... | collective-permute-start | bytes 786440 | tf_op jit(solution)/shard_map/ppermute | solution.py:342
  30.7 24.5 %copy-start.2 = (s32[2,64]{1,0:T(2,128)S(1)}, s32[2,64]{1,0:T(2,128)}, u32[]{:S(2)}) copy-start(s32[2,64]{1,0:T(2,128)} %parents_ref.1) | copy-start | bytes 1540
  30.7 24.5 %copy-start.3 = (s32[2,8]{1,0:T(2,128)S(1)}, s32[2,8]{1,0:T(2,128)}, u32[]{:S(2)}) copy-start(s32[2,8]{1,0:T(2,128)} %accepted_ref.1) | copy-start | bytes 196
  30.8 26.5 %copy-start.7 = (s32[2]{0:T(128)S(1)}, s32[2]{0:T(128)}, u32[]{:S(2)}) copy-start(s32[2]{0:T(128)} %param.18) | copy-start | bytes 28
  34.0 31.5 %collective-permute-start.14 = (bf16[128,1024]{1,0:T(8,128)(2,1)S(1)}, bf16[128,1024]{1,0:T(8,128)(2,1)S(1)}, u32[]{:S(2)}, u32[]{:S(2)}) collective-permute-start(bf16[128,1024]{1,0:T(8,128)(2,1)S(1)} %get-tuple-element.19.refs_1_), channel_id=1, source_target_pairs={{0,24},{8,16},{16,8},{24,0},{1,25},{9,17},{17,9},{25,1},{2,26},{10... | collective-permute-start | bytes 786440 | tf_op jit(solution)/shard_map/ppermute | solution.py:342
  43.0 33.2 %collective-permute-start.1 = (bf16[2,32,5376]{2,1,0:T(8,128)(2,1)S(1)}, bf16[2,32,5376]{2,1,0:T(8,128)(2,1)S(1)}, u32[]{:S(2)}, u32[]{:S(2)}) collective-permute-start(bf16[2,32,5376]{2,1,0:T(8,128)(2,1)S(1)} %slice.160), channel_id=1, source_target_pairs={{0,2},{1,5},{2,0},{3,7},{4,6},{5,1},{6,4},{7,3},{8,10},{9,13},{10,... | collective-permute-start | bytes 2064392 | tf_op jit(solution)/shard_map/ppermute | solution.py:367
  55.2 22.8 %collective-permute-start.6 = (bf16[3,64,5376]{2,1,0:T(8,128)(2,1)S(1)}, bf16[3,64,5376]{2,1,0:T(8,128)(2,1)S(1)}, u32[]{:S(2)}, u32[]{:S(2)}) collective-permute-start(bf16[3,64,5376]{2,1,0:T(8,128)(2,1)S(1)} %bitcast.48), channel_id=1, source_target_pairs={{0,1},{1,0},{2,3},{3,2},{4,5},{5,4},{6,7},{7,6},{8,9},{9,8},{10,11... | collective-permute-start | bytes 6193160 | tf_op jit(solution)/shard_map/ppermute | solution.py:367
  76.2 4.3 %collective-permute-start.15 = (bf16[3,64,5376]{2,1,0:T(8,128)(2,1)S(1)}, bf16[3,64,5376]{2,1,0:T(8,128)(2,1)S(1)}, u32[]{:S(2)}, u32[]{:S(2)}) collective-permute-start(bf16[3,64,5376]{2,1,0:T(8,128)(2,1)S(1)} %bitcast.49), channel_id=1, source_target_pairs={{0,1},{1,0},{2,3},{3,2},{4,5},{5,4},{6,7},{7,6},{8,9},{9,8},{10,11... | collective-permute-start | bytes 6193160 | tf_op jit(solution)/shard_map/ppermute | solution.py:367
  76.4 9.6 %collective-permute-start.2 = (bf16[2,16,5376]{2,1,0:T(8,128)(2,1)S(1)}, bf16[2,16,5376]{2,1,0:T(8,128)(2,1)S(1)}, u32[]{:S(2)}, u32[]{:S(2)}) collective-permute-start(bf16[2,16,5376]{2,1,0:T(8,128)(2,1)S(1)} %slice.163), channel_id=1, source_target_pairs={{0,4},{1,3},{2,6},{3,1},{4,0},{5,7},{6,2},{7,5},{8,12},{9,11},{10,... | collective-permute-start | bytes 1032200 | tf_op jit(solution)/shard_map/ppermute | solution.py:367
  78.4 2.2 %copy-start.6 = (f32[192,5376]{1,0:T(8,128)S(1)}, f32[192,5376]{1,0:T(8,128)}, u32[]{:S(2)}) copy-start(f32[192,5376]{1,0:T(8,128)} %get-tuple-element.27) | copy-start | bytes 12386308
  79.0 15.3 %collective-permute-start.7 = (bf16[3,32,5376]{2,1,0:T(8,128)(2,1)S(1)}, bf16[3,32,5376]{2,1,0:T(8,128)(2,1)S(1)}, u32[]{:S(2)}, u32[]{:S(2)}) collective-permute-start(bf16[3,32,5376]{2,1,0:T(8,128)(2,1)S(1)} %slice.159), channel_id=1, source_target_pairs={{0,2},{1,5},{2,0},{3,7},{4,6},{5,1},{6,4},{7,3},{8,10},{9,13},{10,... | collective-permute-start | bytes 3096584 | tf_op jit(solution)/shard_map/ppermute | solution.py:367
  81.1 29.9 %collective-permute-start.16 = (bf16[3,32,5376]{2,1,0:T(8,128)(2,1)S(1)}, bf16[3,32,5376]{2,1,0:T(8,128)(2,1)S(1)}, u32[]{:S(2)}, u32[]{:S(2)}) collective-permute-start(bf16[3,32,5376]{2,1,0:T(8,128)(2,1)S(1)} %slice.158), channel_id=1, source_target_pairs={{0,2},{1,5},{2,0},{3,7},{4,6},{5,1},{6,4},{7,3},{8,10},{9,13},{10,... | collective-permute-start | bytes 3096584 | tf_op jit(solution)/shard_map/ppermute | solution.py:367
  94.6 18.2 %collective-permute-start.8 = (bf16[3,16,5376]{2,1,0:T(8,128)(2,1)S(1)}, bf16[3,16,5376]{2,1,0:T(8,128)(2,1)S(1)}, u32[]{:S(2)}, u32[]{:S(2)}) collective-permute-start(bf16[3,16,5376]{2,1,0:T(8,128)(2,1)S(1)} %slice.162), channel_id=1, source_target_pairs={{0,4},{1,3},{2,6},{3,1},{4,0},{5,7},{6,2},{7,5},{8,12},{9,11},{10,... | collective-permute-start | bytes 1548296 | tf_op jit(solution)/shard_map/ppermute | solution.py:367
  111.1 9.2 %collective-permute-start.17 = (bf16[3,16,5376]{2,1,0:T(8,128)(2,1)S(1)}, bf16[3,16,5376]{2,1,0:T(8,128)(2,1)S(1)}, u32[]{:S(2)}, u32[]{:S(2)}) collective-permute-start(bf16[3,16,5376]{2,1,0:T(8,128)(2,1)S(1)} %slice.161), channel_id=1, source_target_pairs={{0,4},{1,3},{2,6},{3,1},{4,0},{5,7},{6,2},{7,5},{8,12},{9,11},{10,... | collective-permute-start | bytes 1548296 | tf_op jit(solution)/shard_map/ppermute | solution.py:367
  132.3 14.1 %collective-permute-start.9 = (bf16[1,4,16,1792]{3,2,1,0:T(8,128)(2,1)S(1)}, bf16[1,4,16,1792]{3,2,1,0:T(8,128)(2,1)S(1)}, u32[]{:S(2)}, u32[]{:S(2)}) collective-permute-start(bf16[1,4,16,1792]{3,2,1,0:T(8,128)(2,1)S(1)} %bitcast.42), channel_id=1, source_target_pairs={{0,4},{1,3},{2,6},{3,1},{4,0},{5,7},{6,2},{7,5},{8,12},{9,11},{10,... | collective-permute-start | bytes 688136 | tf_op jit(solution)/shard_map/ppermute | solution.py:385
  145.7 8.6 %collective-permute-start.18 = (bf16[1,4,16,1792]{3,2,1,0:T(8,128)(2,1)S(1)}, bf16[1,4,16,1792]{3,2,1,0:T(8,128)(2,1)S(1)}, u32[]{:S(2)}, u32[]{:S(2)}) collective-permute-start(bf16[1,4,16,1792]{3,2,1,0:T(8,128)(2,1)S(1)} %bitcast.38), channel_id=1, source_target_pairs={{0,4},{1,3},{2,6},{3,1},{4,0},{5,7},{6,2},{7,5},{8,12},{9,11},{10,... | collective-permute-start | bytes 688136 | tf_op jit(solution)/shard_map/ppermute | solution.py:385
  146.4 8.5 %collective-permute-start.10 = (bf16[2,4,16,1792]{3,2,1,0:T(8,128)(2,1)S(1)}, bf16[2,4,16,1792]{3,2,1,0:T(8,128)(2,1)S(1)}, u32[]{:S(2)}, u32[]{:S(2)}) collective-permute-start(bf16[2,4,16,1792]{3,2,1,0:T(8,128)(2,1)S(1)} %pad_maximum_fusion.6), channel_id=1, source_target_pairs={{0,2},{1,5},{2,0},{3,7},{4,6},{5,1},{6,4},{7,3},{8,10},{9,13},{10,... | collective-permute-start | bytes 1376264 | tf_op jit(solution)/shard_map/ppermute | solution.py:385
  154.4 8.5 %collective-permute-start.19 = (bf16[2,4,16,1792]{3,2,1,0:T(8,128)(2,1)S(1)}, bf16[2,4,16,1792]{3,2,1,0:T(8,128)(2,1)S(1)}, u32[]{:S(2)}, u32[]{:S(2)}) collective-permute-start(bf16[2,4,16,1792]{3,2,1,0:T(8,128)(2,1)S(1)} %pad_maximum_fusion.7), channel_id=1, source_target_pairs={{0,2},{1,5},{2,0},{3,7},{4,6},{5,1},{6,4},{7,3},{8,10},{9,13},{10,... | collective-permute-start | bytes 1376264 | tf_op jit(solution)/shard_map/ppermute | solution.py:385
  155.0 8.8 %collective-permute-start.11 = (bf16[4,4,16,1792]{3,2,1,0:T(8,128)(2,1)S(1)}, bf16[4,4,16,1792]{3,2,1,0:T(8,128)(2,1)S(1)}, u32[]{:S(2)}, u32[]{:S(2)}) collective-permute-start(bf16[4,4,16,1792]{3,2,1,0:T(8,128)(2,1)S(1)} %pad_maximum_fusion.2), channel_id=1, source_target_pairs={{0,1},{1,0},{2,3},{3,2},{4,5},{5,4},{6,7},{7,6},{8,9},{9,8},{10,11... | collective-permute-start | bytes 2752520 | tf_op jit(solution)/shard_map/ppermute | solution.py:385
  163.0 6.2 %collective-permute-start.20 = (bf16[4,4,16,1792]{3,2,1,0:T(8,128)(2,1)S(1)}, bf16[4,4,16,1792]{3,2,1,0:T(8,128)(2,1)S(1)}, u32[]{:S(2)}, u32[]{:S(2)}) collective-permute-start(bf16[4,4,16,1792]{3,2,1,0:T(8,128)(2,1)S(1)} %pad_maximum_fusion.3), channel_id=1, source_target_pairs={{0,1},{1,0},{2,3},{3,2},{4,5},{5,4},{6,7},{7,6},{8,9},{9,8},{10,11... | collective-permute-start | bytes 2752520 | tf_op jit(solution)/shard_map/ppermute | solution.py:385
  174.6 13.9 %collective-permute-start.21 = (bf16[448,128]{1,0:T(8,128)(2,1)S(1)}, bf16[448,128]{1,0:T(8,128)(2,1)S(1)}, u32[]{:S(2)}, u32[]{:S(2)}) collective-permute-start(bf16[448,128]{1,0:T(8,128)(2,1)S(1)} %get-tuple-element.39), channel_id=1, source_target_pairs={{0,8},{8,0},{16,24},{24,16},{1,9},{9,1},{17,25},{25,17},{2,10},{10... | collective-permute-start | bytes 344072 | tf_op jit(solution)/shard_map/ppermute | solution.py:342
  182.9 11.8 %collective-permute-start.22 = (bf16[448,128]{1,0:T(8,128)(2,1)S(1)}, bf16[448,128]{1,0:T(8,128)(2,1)S(1)}, u32[]{:S(2)}, u32[]{:S(2)}) collective-permute-start(bf16[448,128]{1,0:T(8,128)(2,1)S(1)} %get-tuple-element.38), channel_id=1, source_target_pairs={{0,16},{8,24},{16,0},{24,8},{1,17},{9,25},{17,1},{25,9},{2,18},{10... | collective-permute-start | bytes 344072 | tf_op jit(solution)/shard_map/ppermute | solution.py:342
  183.9 10.8 %collective-permute-start.23 = (bf16[448,128]{1,0:T(8,128)(2,1)S(1)}, bf16[448,128]{1,0:T(8,128)(2,1)S(1)}, u32[]{:S(2)}, u32[]{:S(2)}) collective-permute-start(bf16[448,128]{1,0:T(8,128)(2,1)S(1)} %get-tuple-element.37), channel_id=1, source_target_pairs={{0,24},{8,16},{16,8},{24,0},{1,25},{9,17},{17,9},{25,1},{2,26},{10... | collective-permute-start | bytes 344072 | tf_op jit(solution)/shard_map/ppermute | solution.py:342
  185.4 9.3 %collective-permute-start.24 = (bf16[448,128]{1,0:T(8,128)(2,1)S(1)}, bf16[448,128]{1,0:T(8,128)(2,1)S(1)}, u32[]{:S(2)}, u32[]{:S(2)}) collective-permute-start(bf16[448,128]{1,0:T(8,128)(2,1)S(1)} %get-tuple-element.36), channel_id=1, source_target_pairs={{0,8},{8,0},{16,24},{24,16},{1,9},{9,1},{17,25},{25,17},{2,10},{10... | collective-permute-start | bytes 344072 | tf_op jit(solution)/shard_map/ppermute | solution.py:342
  186.5 18.0 %collective-permute-start.25 = (bf16[448,128]{1,0:T(8,128)(2,1)S(1)}, bf16[448,128]{1,0:T(8,128)(2,1)S(1)}, u32[]{:S(2)}, u32[]{:S(2)}) collective-permute-start(bf16[448,128]{1,0:T(8,128)(2,1)S(1)} %get-tuple-element.35), channel_id=1, source_target_pairs={{0,16},{8,24},{16,0},{24,8},{1,17},{9,25},{17,1},{25,9},{2,18},{10... | collective-permute-start | bytes 344072 | tf_op jit(solution)/shard_map/ppermute | solution.py:342
  188.5 16.1 %collective-permute-start.26 = (bf16[448,128]{1,0:T(8,128)(2,1)S(1)}, bf16[448,128]{1,0:T(8,128)(2,1)S(1)}, u32[]{:S(2)}, u32[]{:S(2)}) collective-permute-start(bf16[448,128]{1,0:T(8,128)(2,1)S(1)} %get-tuple-element.34), channel_id=1, source_target_pairs={{0,24},{8,16},{16,8},{24,0},{1,25},{9,17},{17,9},{25,1},{2,26},{10... | collective-permute-start | bytes 344072 | tf_op jit(solution)/shard_map/ppermute | solution.py:342
  (3 other events, 5.8 us)

commit v2 on v0

--- a/solution.py
+++ b/solution.py
@@ -1,10 +1,631 @@
+import functools
+
 import jax
 import jax.numpy as jnp
 from jax import lax
+from jax.experimental import pallas as pl
+from jax.experimental.pallas import tpu as pltpu
 from jax.sharding import PartitionSpec as P
 
 HEAD_SIZE = 224
 NODES = 64
+LANES = 128
+F32 = jnp.float32
+BF16 = jnp.bfloat16
+SMALL = pl.CostEstimate(flops=1, bytes_accessed=1, transcendentals=0)
+LARGE = pl.CostEstimate(flops=2 * 10**11, bytes_accessed=1, transcendentals=0)
+
+
+def dot(a, b, dims=((1,), (0,))):
+    return lax.dot_general(a, b, (dims, ((), ())), preferred_element_type=F32)
+
+
+def whole(shape):
+    return pl.BlockSpec(shape, lambda *_: (0,) * len(shape))
+
+
+def ordered(kernel, after, operands, in_specs, megabytes, cost=SMALL, **options):
+    count = len(after)
+
+    def body(*refs):
+        kernel(*refs[count:])
+
+    return pl.pallas_call(
+        body,
+        in_specs=[pl.BlockSpec(memory_space=pl.ANY)] * count + in_specs,
+        compiler_params=pltpu.CompilerParams(vmem_limit_bytes=megabytes * 2**20),
+        cost_estimate=cost,
+        **options,
+    )(*after, *operands)
+
+
+def row_to_column(row):
+    size = row.shape[1]
+    eye = lax.broadcasted_iota(jnp.int32, (size, size), 0) == lax.broadcasted_iota(
+        jnp.int32, (size, size), 1
+    )
+    return jnp.sum(jnp.where(eye, row, 0), axis=1, keepdims=True)
+
+
+def rank_in_plane(row):
+    before = row_to_column(row) < row
+    return jnp.sum(before.astype(jnp.int32), axis=0, keepdims=True)
+
+
+def plane_row(ids_ref, plane, rows):
+    per = rows // LANES
+    parts = [ids_ref[pl.ds(plane * per + i, 1), :] for i in range(per)]
+    return jnp.concatenate(parts, axis=1)
+
+
+CHUNK = 32
+
+
+def norm_kernel(slots, rank_rows, ids_ref, stream_hbm, gain_ref, down_hbm, first_ref, second_ref,
+                place_ref, normed, held, down_ref, arrived, down_arrived):
+    me = lax.axis_index("head")
+    plane = lax.axis_index("tok")
+    rows, width = held.shape
+    copies = [
+        pltpu.make_async_copy(
+            stream_hbm.at[pl.ds(i * CHUNK, CHUNK), :],
+            held.at[pl.ds(i * CHUNK, CHUNK), :],
+            arrived.at[i],
+        )
+        for i in range(rows // CHUNK)
+    ]
+    for copy in copies:
+        copy.start()
+    down_copy = pltpu.make_async_copy(down_hbm, down_ref, down_arrived)
+    down_copy.start()
+    gains = gain_ref[...].astype(F32)
+    gain = jnp.concatenate([gains[i : i + 1] for i in range(width // LANES)], axis=1)
+
+    def norm(i, carry):
+        at = pl.ds(pl.multiple_of(i * CHUNK, CHUNK), CHUNK)
+        pltpu.make_async_copy(stream_hbm.at[at, :], held.at[at, :], arrived.at[i]).wait()
+        wide = held[at, :].astype(F32)
+        rstd = lax.rsqrt(jnp.sum(wide * wide, axis=1, keepdims=True) / width + 1e-05)
+        normed[at, :] = (wide * rstd * gain).astype(BF16)
+        return carry
+
+    lax.fori_loop(0, rows // CHUNK, norm, 0)
+    down_copy.wait()
+    low = dot(normed[...], down_ref[...]).astype(BF16)
+    ranks = low.shape[1]
+    lane = lax.broadcasted_iota(jnp.int32, (ranks, LANES), 1)
+    wanted = jnp.where(lane < rank_rows, me * rank_rows + lane, (me ^ 1) * rank_rows + lane - rank_rows)
+    pick = lax.broadcasted_iota(jnp.int32, (ranks, LANES), 0) == wanted
+    pick &= lane < 2 * rank_rows
+    low = dot(low, pick.astype(BF16)).astype(BF16)
+    ids = plane_row(ids_ref, plane, rows)
+    rank = rank_in_plane(ids)
+    owner = ids // (2 * NODES)
+    second = (ids // NODES) % 2
+    apart = owner ^ me
+    even = (owner & 1) == 0
+    bit_x = (apart >> 1) & 1
+    bit_y = (apart >> 2) & 1
+    order = (apart & 1) * 4 + jnp.where(even, bit_x * 2 + bit_y, bit_y * 2 + bit_x)
+    half = rows // 2
+    position = second * half + order * slots + rank % slots
+    place_ref[...] = (
+        lax.broadcasted_iota(jnp.int32, (rows, rows), 0) == position
+    ).astype(BF16)
+    quarter = half // 2
+    position = jnp.where(order < 4, second * quarter + order * slots + rank % slots, -1)
+    place = (lax.broadcasted_iota(jnp.int32, (half, rows), 0) == position).astype(BF16)
+    columns = (first_ref.shape[1] - LANES) // 2
+    for i, owner_of in enumerate((me, me ^ 1)):
+        block = normed[:, pl.ds(pl.multiple_of(owner_of * columns, LANES), columns)]
+        sorted_block = dot(place, block).astype(BF16)
+        first_ref[:, i * columns : (i + 1) * columns] = sorted_block[:quarter]
+        second_ref[:, i * columns : (i + 1) * columns] = sorted_block[quarter:]
+    sorted_low = dot(place, low).astype(BF16)
+    first_ref[:, 2 * columns :] = sorted_low[:quarter]
+    second_ref[:, 2 * columns :] = sorted_low[quarter:]
+
+
+def prep_kernel(slots, planes, rows, ids_ref, parents_ref, accepted_ref, mask_ref, chosen_ref):
+    me = lax.axis_index("head")
+    plane = lax.axis_index("tok")
+    for j in range(2):
+        nodes = []
+        for k in range(planes):
+            ids = plane_row(ids_ref, plane ^ k, rows)
+            rank = rank_in_plane(ids)
+            spot = lax.broadcasted_iota(jnp.int32, (slots, rows), 0) + (me * 2 + j) * slots
+            nodes.append(
+                jnp.sum(jnp.where(rank == spot, ids, 0), axis=1, keepdims=True)
+                - (me * 2 + j) * NODES
+            )
+        nodes = jnp.concatenate(nodes, axis=0)
+        lanes = lax.broadcasted_iota(jnp.int32, (NODES, NODES), 1)
+        rows_of = lax.broadcasted_iota(jnp.int32, (NODES, NODES), 0)
+        named = (nodes == lanes).astype(BF16)
+        parent = row_to_column(parents_ref[j : j + 1, :])
+        reach = ((parent == lanes) | (rows_of == lanes)).astype(BF16)
+        for _ in range((NODES - 1).bit_length()):
+            reach = jnp.minimum(dot(reach, reach), 1.0).astype(BF16)
+        mask_ref[j] = dot(dot(named, reach).astype(BF16), named, ((1,), (1,)))
+        accepted = row_to_column(accepted_ref[j : j + 1, :])
+        depth = accepted.shape[0]
+        wanted = (accepted == lax.broadcasted_iota(jnp.int32, (depth, NODES), 1)).astype(BF16)
+        chosen_ref[j] = dot(wanted, named, ((1,), (1,)))
+
+
+def tiles_of(width):
+    first = (width // 512 + 1) * 256 if width % 512 else width // 2
+    return [(0, first), (first, width - first)]
+
+
+def project_kernel(pieces, *refs):
+    lhs_refs = refs[:pieces]
+    weight_refs = refs[pieces : pieces + 2]
+    up_refs = refs[pieces + 2 : pieces + 4]
+    keep_hbm, send_hbm = refs[pieces + 4 : pieces + 6]
+    lhs, held, keep, send, arrived, left = refs[-6:]
+    parts, columns, width = weight_refs[0].shape
+    deep = held.shape[1]
+    half = lhs.shape[0] // 2
+    rank_rows = up_refs[0].shape[1]
+    steps = [(p, start, size) for p in range(parts) for start, size in tiles_of(width)]
+
+    def inward(i, side):
+        p, start, size = steps[i]
+        return pltpu.make_async_copy(
+            weight_refs[side].at[p, :, pl.ds(start, size)],
+            held.at[p, pl.ds(side * columns, columns), pl.ds(start, size)],
+            arrived.at[i, side],
+        )
+
+    for i in range(len(steps)):
+        for side in range(2):
+            inward(i, side).start()
+    at = 0
+    for lhs_ref in lhs_refs:
+        rows = lhs_ref.shape[0] // 2
+        lhs[at : at + rows, :] = lhs_ref[:rows, :]
+        lhs[half + at : half + at + rows, :] = lhs_ref[rows:, :]
+        at += rows
+    for p in range(parts):
+        low = 2 * columns
+        for side in range(2):
+            held[p, low : low + rank_rows, :] = up_refs[side][p]
+            low += rank_rows
+        held[p, low:, :] = jnp.zeros((deep - low, width), BF16)
+    outward = []
+    for i, (p, start, size) in enumerate(steps):
+        for side in range(2):
+            inward(i, side).wait()
+        lanes = slice(p * width + start, p * width + start + size)
+        total = dot(lhs[...], held[p, :, start : start + size])
+        keep[:, lanes] = total[:half]
+        send[:, lanes] = total[half:].astype(BF16)
+        for j, (source, target) in enumerate(((keep, keep_hbm), (send, send_hbm))):
+            copy = pltpu.make_async_copy(source.at[:, lanes], target.at[:, lanes], left.at[i, j])
+            copy.start()
+            outward.append(copy)
+    for copy in outward:
+        copy.wait()
+
+
+def project(pieces, weights, ups, after=()):
+    parts, columns, width = weights[0].shape
+    steps = parts * len(tiles_of(width))
+    rows = sum(piece.shape[0] for piece in pieces) // 2
+    deep = pieces[0].shape[1]
+    far = pl.BlockSpec(memory_space=pltpu.HBM)
+    return ordered(
+        functools.partial(project_kernel, len(pieces)),
+        after,
+        (*pieces, *weights, *ups),
+        [whole(piece.shape) for piece in pieces] + [far] * 2 + [whole(ups[0].shape)] * 2,
+        58,
+        LARGE,
+        out_specs=[far] * 2,
+        out_shape=[
+            jax.ShapeDtypeStruct((rows, parts * width), F32),
+            jax.ShapeDtypeStruct((rows, parts * width), BF16),
+        ],
+        scratch_shapes=[
+            pltpu.VMEM((2 * rows, deep), BF16),
+            pltpu.VMEM((parts, deep, width), BF16),
+            pltpu.VMEM((rows, parts * width), F32),
+            pltpu.VMEM((rows, parts * width), BF16),
+            pltpu.SemaphoreType.DMA((steps, 2)),
+            pltpu.SemaphoreType.DMA((steps, 2)),
+        ],
+    )
+
+
+def halve_kernel(keep_ref, got_ref, kept_ref, send_ref):
+    added = keep_ref[...] + got_ref[...].astype(F32)
+    half = added.shape[1] // 2
+    kept_ref[...] = added[:, :half]
+    send_ref[...] = added[:, half:].astype(BF16)
+
+
+def halve(keep, got, parts, after=()):
+    batch, rows, wide = keep.shape
+    tile = wide // parts
+    half = rows // 2
+
+    def block(rows):
+        return pl.BlockSpec((batch, rows, tile), lambda c: (0, 0, c))
+
+    return ordered(
+        halve_kernel,
+        after,
+        (keep, got),
+        [block(rows)] * 2,
+        16,
+        grid=(parts,),
+        out_specs=[block(half)] * 2,
+        out_shape=[
+            jax.ShapeDtypeStruct((batch, half, wide), F32),
+            jax.ShapeDtypeStruct((batch, half, wide), BF16),
+        ],
+    )
+
+
+def join_kernel(own_keep_ref, own_got_ref, keep_ref, got_ref, out_ref):
+    slots = own_keep_ref.shape[0]
+    out_ref[:slots] = (own_keep_ref[...] + own_got_ref[...].astype(F32)).astype(BF16)
+    for k in range(keep_ref.shape[0]):
+        out_ref[(k + 1) * slots : (k + 2) * slots] = (
+            keep_ref[k] + got_ref[k].astype(F32)
+        ).astype(BF16)
+
+
+def join(j, own, rest, parts, after=()):
+    batch, slots, wide = rest[0].shape
+    tile = wide // parts
+    near = pl.BlockSpec((None, slots, tile), lambda c: (j, 0, c))
+    far = pl.BlockSpec((batch, slots, tile), lambda c: (0, 0, c))
+    return ordered(
+        join_kernel,
+        after,
+        (*own, *rest),
+        [near, near, far, far],
+        16,
+        grid=(parts,),
+        out_specs=pl.BlockSpec(((batch + 1) * slots, tile), lambda c: (0, c)),
+        out_shape=jax.ShapeDtypeStruct(((batch + 1) * slots, wide), BF16),
+    )
+
+
+HEADS = 4
+LOG2E = 1.4426950408889634
+
+
+def attend_kernel(j, span, groups, length_ref, triple_ref, mask_ref, chosen_ref, cache_ref,
+                  out_ref, kept_ref, spread, top, total, acc, held, arrived):
+    chunks = held.shape[1]
+    tile = spread.shape[2]
+    width = groups * tile
+    length = length_ref[j]
+    scale = HEAD_SIZE ** (-0.5) * LOG2E
+
+    def copy(part, c):
+        return pltpu.make_async_copy(
+            cache_ref.at[part, j, pl.ds(c * span, span), :], held.at[part, c], arrived.at[part, c]
+        )
+
+    for c in range(chunks):
+        @pl.when(c * span < length)
+        def fetch():
+            copy(0, c).start()
+            copy(1, c).start()
+
+    head_of_lane = lax.broadcasted_iota(jnp.int32, (1, tile), 1) // HEAD_SIZE
+
+    def fold(g, scores, values, first):
+        peak = jnp.max(scores, axis=1, keepdims=True)
+        if not first:
+            before = top[g]
+            peak = jnp.maximum(before, peak)
+        weights = jnp.exp2(scores - peak)
+        gained = jnp.sum(weights, axis=1, keepdims=True)
+        part = dot(weights.astype(BF16), values)
+        if first:
+            total[g] = gained
+            acc[g] = part
+        else:
+            shrink = jnp.exp2(before - peak)
+            total[g] = total[g] * shrink + gained
+            acc[g] = acc[g] * shrink + part
+        top[g] = peak
+
+    allowed = jnp.concatenate([mask_ref[j]] * HEADS, axis=0) > 0.5
+    pick = chosen_ref[j].astype(BF16)
+    for g in range(groups):
+        lanes = slice(g * tile, (g + 1) * tile)
+        query = triple_ref[:, lanes]
+        keys = triple_ref[:, width + g * tile : width + (g + 1) * tile]
+        values = triple_ref[:, 2 * width + g * tile : 2 * width + (g + 1) * tile]
+        for h in range(HEADS):
+            spread[g, h * NODES : (h + 1) * NODES, :] = jnp.where(head_of_lane == h, query, 0)
+        scores = dot(spread[g], keys, ((1,), (1,))) * scale
+        fold(g, jnp.where(allowed, scores, -1e30), values, True)
+        kept_ref[0, :, lanes] = dot(pick, keys).astype(BF16)
+        kept_ref[1, :, lanes] = dot(pick, values).astype(BF16)
+
+    for c in range(chunks):
+        @pl.when(c * span < length)
+        def cached():
+            copy(0, c).wait()
+            copy(1, c).wait()
+            spot = lax.broadcasted_iota(jnp.int32, (1, span), 1) + c * span
+            bias = jnp.where(spot < length, 0.0, -1e30)
+            for g in range(groups):
+                lanes = slice(g * tile, (g + 1) * tile)
+                scores = dot(spread[g], held[0, c, :, lanes], ((1,), (1,)))
+                fold(g, scores * scale + bias, held[1, c, :, lanes], False)
+
+    for g in range(groups):
+        share = acc[g] / total[g]
+        out = jnp.zeros((NODES, tile), F32)
+        for h in range(HEADS):
+            out = jnp.where(head_of_lane == h, share[h * NODES : (h + 1) * NODES, :], out)
+        out_ref[:, g * tile : (g + 1) * tile] = out.astype(BF16)
+
+
+def attend(j, lengths, triple, masks, chosen, cache, after=()):
+    cache_span, width = cache.shape[2:]
+    tile = HEADS * HEAD_SIZE
+    groups = width // tile
+    span = min(512, cache_span)
+    chunks = cache_span // span
+    depth = chosen.shape[1]
+    return ordered(
+        functools.partial(attend_kernel, j, span, groups),
+        after,
+        (lengths, triple, masks, chosen, cache),
+        [
+            pl.BlockSpec(memory_space=pltpu.SMEM),
+            whole(triple.shape),
+            whole(masks.shape),
+            whole(chosen.shape),
+            pl.BlockSpec(memory_space=pltpu.HBM),
+        ],
+        32,
+        out_specs=[whole((NODES, width)), whole((2, depth, width))],
+        out_shape=[
+            jax.ShapeDtypeStruct((NODES, width), BF16),
+            jax.ShapeDtypeStruct((2, depth, width), BF16),
+        ],
+        scratch_shapes=[
+            pltpu.VMEM((groups, HEADS * NODES, tile), BF16),
+            pltpu.VMEM((groups, HEADS * NODES, 1), F32),
+            pltpu.VMEM((groups, HEADS * NODES, 1), F32),
+            pltpu.VMEM((groups, HEADS * NODES, tile), F32),
+            pltpu.VMEM((2, chunks, span, width), BF16),
+            pltpu.SemaphoreType.DMA((2, chunks)),
+        ],
+    )
+
+
+def pack_kernel(*refs):
+    rows = refs[0].shape[0]
+    for i, ref in enumerate(refs[:-1]):
+        refs[-1][i * rows : (i + 1) * rows, :] = ref[...]
+
+
+def pack(pieces, after=()):
+    rows, width = pieces[0].shape
+    return ordered(
+        pack_kernel,
+        after,
+        pieces,
+        [whole((rows, width))] * len(pieces),
+        16,
+        out_shape=jax.ShapeDtypeStruct((rows * len(pieces), width), BF16),
+    )
+
+
+def lift_kernel(planes, slots, *refs):
+    pieces = refs[:-4]
+    weight_ref, own_ref, other_ref, rows = refs[-4:]
+    share = rows.shape[0] // planes
+    for k in range(planes):
+        at = k * share
+        for piece in pieces:
+            for q in range(piece.shape[0] // (planes * slots)):
+                rows[at : at + slots, :] = piece[
+                    (q * planes + k) * slots : (q * planes + k + 1) * slots, :
+                ]
+                at += slots
+    lifted = dot(weight_ref[...], rows[...], ((1,), (1,)))
+    for k in range(planes):
+        piece = lifted[:, k * share : (k + 1) * share]
+        if k % 2 == 0:
+            own_ref[k // 2] = piece
+        else:
+            other_ref[k // 2] = piece.astype(BF16)
+
+
+def lift(pieces, planes, slots, weight, after=()):
+    wide, width = weight.shape
+    rows = sum(piece.shape[0] for piece in pieces)
+    return ordered(
+        functools.partial(lift_kernel, planes, slots),
+        after,
+        (*pieces, weight),
+        [whole(piece.shape) for piece in pieces] + [whole(weight.shape)],
+        20,
+        out_shape=[
+            jax.ShapeDtypeStruct((planes // 2, wide, rows // planes), F32),
+            jax.ShapeDtypeStruct((planes // 2, wide, rows // planes), BF16),
+        ],
+        scratch_shapes=[pltpu.VMEM((rows, width), BF16)],
+    )
+
+
+def settle_kernel(own_ref, got_ref, kept_ref, send_ref, *_):
+    kept_ref[...] = own_ref[0] + got_ref[0].astype(F32)
+    send_ref[...] = (own_ref[1] + got_ref[1].astype(F32)).astype(BF16)
+
+
+def settle(own, got, passed=()):
+    shape = own.shape[1:]
+    return ordered(
+        settle_kernel,
+        passed,
+        (own, got),
+        [whole(own.shape)] * 2,
+        16,
+        out_specs=[whole(shape)] * 2 + [pl.BlockSpec(memory_space=pl.ANY)] * len(passed),
+        out_shape=[jax.ShapeDtypeStruct(shape, F32), jax.ShapeDtypeStruct(shape, BF16)]
+        + [jax.ShapeDtypeStruct(array.shape, array.dtype) for array in passed],
+        input_output_aliases={i: 2 + i for i in range(len(passed))},
+    )
+
+
+def final_kernel(place_ref, *refs):
+    sums = [
+        (refs[2 * j][...] + refs[2 * j + 1][...].astype(F32)).astype(BF16) for j in range(2)
+    ]
+    refs[-1][...] = dot(jnp.concatenate(sums, axis=1), place_ref[...]).astype(BF16)
+
+
+def on_device(
+    stream,
+    row_tree_nodes,
+    input_norm_gain,
+    query_key_value_weight,
+    adapter_down_weight,
+    adapter_up_weight,
+    key_value_cache,
+    cache_length,
+    parents,
+    accepted,
+    output_weight,
+):
+    rows, width_in = stream.shape
+    planes = row_tree_nodes.shape[0] // rows
+    owners = width_in // query_key_value_weight.shape[0]
+    slots = rows // (2 * owners)
+    columns = query_key_value_weight.shape[0]
+    width = query_key_value_weight.shape[2]
+    rank_rows = adapter_up_weight.shape[0]
+    weight = jnp.swapaxes(query_key_value_weight, 0, 1)
+    up = jnp.swapaxes(adapter_up_weight, 0, 1)
+    down = jnp.swapaxes(output_weight, 0, 1)
+    ids = row_tree_nodes.reshape(-1, LANES)
+
+    def first_mask(h):
+        return 2 if h % 2 == 0 else 4
+
+    core_pairs = [(h, h ^ 1) for h in range(owners)]
+    first_pairs = [(h, h ^ first_mask(h)) for h in range(owners)]
+    second_pairs = [(h, h ^ (6 - first_mask(h))) for h in range(owners)]
+
+    def across(array, k):
+        return lax.ppermute(array, "tok", [(z, z ^ k) for z in range(planes)])
+
+    weights = (weight, lax.ppermute(weight, "head", core_pairs))
+    ups = (up, lax.ppermute(up, "head", core_pairs))
+    feature = jax.ShapeDtypeStruct((rows // 4, 2 * columns + LANES), BF16)
+    first, second, place = ordered(
+        functools.partial(norm_kernel, slots, rank_rows),
+        (),
+        (ids, stream, input_norm_gain.reshape(-1, LANES), adapter_down_weight),
+        [whole(ids.shape), pl.BlockSpec(memory_space=pltpu.HBM),
+         whole((width_in // LANES, LANES)), pl.BlockSpec(memory_space=pltpu.HBM)],
+        58,
+        out_shape=[feature, feature, jax.ShapeDtypeStruct((rows, rows), BF16)],
+        scratch_shapes=[
+            pltpu.VMEM((rows, width_in), BF16),
+            pltpu.VMEM((rows, width_in), BF16),
+            pltpu.VMEM(adapter_down_weight.shape, BF16),
+            pltpu.SemaphoreType.DMA((rows // CHUNK,)),
+            pltpu.SemaphoreType.DMA,
+        ],
+    )
+    near = [first, second]
+
+    def swap(send, pairs, batch):
+        return lax.ppermute(send.reshape(batch, -1, send.shape[-1]), "head", pairs)
+
+    def split(keep, got, batch, after):
+        return halve(keep.reshape(batch, -1, keep.shape[-1]), got, 3, after)
+
+    rest = planes - 1
+
+    def relay(piece, after):
+        return ordered(
+            pack_kernel,
+            after,
+            (piece,),
+            [whole(piece.shape)],
+            16,
+            out_shape=jax.ShapeDtypeStruct(piece.shape, BF16),
+        )
+
+    beside, beyond = across(first, 1), across(first, 2)
+    own_keep, own_send = project(near, weights, ups)
+    far0 = [beside, beyond, across(relay(beyond, (own_send, beside)), 1)]
+    later = relay(second, (far0[2],))
+    beside, beyond = across(later, 1), across(later, 2)
+    own_got = swap(own_send, first_pairs, 2)
+    keep0, send0 = project(far0, weights, ups, (own_send, later))
+    got0 = swap(send0, first_pairs, rest)
+    own_keep, own_send = split(own_keep, own_got, 2, (send0,))
+    own_got = swap(own_send, second_pairs, 2)
+    depth = accepted.shape[1]
+    masks, chosen = ordered(
+        functools.partial(prep_kernel, slots, planes, rows),
+        (own_send,),
+        (ids, parents, accepted),
+        [whole(ids.shape), whole(parents.shape), whole(accepted.shape)],
+        16,
+        out_shape=[
+            jax.ShapeDtypeStruct((2, NODES, NODES), F32),
+            jax.ShapeDtypeStruct((2, depth, NODES), F32),
+        ],
+    )
+    far1 = [beside, beyond, across(relay(beyond, (send0, beside)), 1)]
+    keep1, send1 = project(far1, weights, ups, (chosen,))
+    got1 = swap(send1, first_pairs, rest)
+    keep0, send0 = split(keep0, got0, rest, (send1,))
+    got0 = swap(send0, second_pairs, rest)
+    keep1, send1 = split(keep1, got1, rest, (send0,))
+    got1 = swap(send1, second_pairs, rest)
+    triple = join(0, (own_keep, own_got), (keep0, got0), 3, (send1,))
+    out0, kept0 = attend(0, cache_length, triple, masks, chosen, key_value_cache)
+
+    def spread_out(out):
+        away_first = lax.ppermute(out, "head", first_pairs)
+        away_second = lax.ppermute(out, "head", second_pairs)
+        away_both = lax.ppermute(out, "head", [(h, h ^ 6) for h in range(owners)])
+        return (out, away_second, away_first, away_both)
+
+    side0 = spread_out(out0)
+    triple = join(1, (own_keep, own_got), (keep1, got1), 3, (out0,))
+    out1, kept1 = attend(1, cache_length, triple, masks, chosen, key_value_cache)
+    side1 = spread_out(out1)
+
+    def other_core(packed):
+        return packed, lax.ppermute(packed, "head", core_pairs)
+
+    own0, away0 = lift(other_core(pack(side0, (out1,))), planes, slots, down)
+    home0 = across(away0, 1)
+    own0, away0, packed = settle(own0, home0, (pack(side1, (own0,)),))
+    home0 = across(away0, 2)
+    own1, away1 = lift(other_core(packed), planes, slots, down)
+    own1, away1 = settle(own1, across(away1, 1))
+    home1 = across(away1, 2)
+    operands = (place, own0, home0, own1, home1)
+    attended = ordered(
+        final_kernel,
+        (),
+        operands,
+        [whole(operand.shape) for operand in operands],
+        16,
+        out_shape=jax.ShapeDtypeStruct((output_weight.shape[1], rows), BF16),
+    )
+    return jnp.swapaxes(attended, 0, 1), jnp.stack([kept0, kept1], axis=1)
 
 
 def ancestors_of(parents):
@@ -18,7 +639,7 @@
     return ancestry
 
 
-def on_device(
+def plain_on_device(
     stream,
     row_tree_nodes,
     input_norm_gain,
@@ -131,8 +752,9 @@
         P("head", None),
         P("tok", "head"),
     )
+    sized = mesh.shape["head"] == 8 and mesh.shape["tok"] == 4
     return jax.shard_map(
-        on_device,
+        on_device if sized else plain_on_device,
         mesh=mesh,
         in_specs=placed,
         out_specs=(P("tok", "head"), P(None, "head", None, "tok")),

time: 360 us -> 160 us (0.44)
  local copies, waits for them, and re-layouts: 114 us -> 3.28 us
  waiting for transfers between devices: 129 us -> 49.5 us
  Pallas kernels: 0 us -> 71.7 us
  matrix products: 67 us -> 0 us
  starting transfers between devices: 0.16 us -> 34.3 us
  blocking collectives: 18.2 us -> 0 us
  other arithmetic: 15.9 us -> 0.01 us
  between operations: 14 us -> 0.98 us
    reduce_scatter x2 -> x0, waiting for transfers between devices: 94.5 us -> none  [the longest x1 74.4 us: on_device(): lax.psum_scatter(part_sum + jnp.dot(gathered_ranks[node_to_row], lifting_...]
    pallas_call x0 -> x22, Pallas kernels: none -> 71.7 us  [ordered(): pl.pallas_call(body, in_specs=[pl.BlockSpec(memory_space=pl.ANY)] * count...]
    dot_general x15 -> x0, matrix products: 67 us -> none  [the longest x1 22.8 us: on_device(): jnp.dot(gathered_features[node_to_row], projection, preferred_element_typ...]
    slice x4 -> x0, local copies, waits for them, and re-layouts: 65.2 us -> none  [the longest x2 45.5 us: on_device(): key_value_cache[1]]
    ppermute x0 -> x26, waiting for transfers between devices: none -> 49.5 us  [the longest x10 18.4 us: across(): return lax.ppermute(array, 'tok', [(z, z ^ k) for z in range(planes)])]
    all_gather x2 -> x0, waiting for transfers between devices: 34.6 us -> none  [the longest x1 34.6 us: on_device(): everything = lax.all_gather(head_rows, 'head', axis=0, tiled=True)]
    ppermute x0 -> x26, starting transfers between devices: none -> 34.3 us  [the longest x10 18.6 us: across(): return lax.ppermute(array, 'tok', [(z, z ^ k) for z in range(planes)])]
    gather x5 -> x0, local copies, waits for them, and re-layouts: 22.7 us -> none  [the longest x1 10.8 us: on_device(): everything[row_tree_nodes]]
  transfers between devices with their start and end apart: 4 -> 26, of which waited for: 3 -> 9; matrix products, arithmetic and copies ran while one was open for 29% -> 0% of each run, Pallas kernels for 0% -> 43%
where the time goes in v2:
time: 160 us
  Pallas kernels  71.7 us (45%)
  waiting for transfers between devices  49.5 us (31%)
  starting transfers between devices  34.3 us (21%)
  local copies, waits for them, and re-layouts  3.28 us (2%)
    pallas_call x22, Pallas kernels, ordered(): pl.pallas_call(body, in_specs=[pl.BlockSpec(memory_space=pl.ANY)] * count...  71.7 us
    ppermute x10, starting transfers between devices, across(): return lax.ppermute(array, 'tok', [(z, z ^ k) for z in range(planes)])  18.6 us
    ppermute x10, waiting for transfers between devices, across(): return lax.ppermute(array, 'tok', [(z, z ^ k) for z in range(planes)])  18.4 us
    ppermute x6, waiting for transfers between devices, swap(): return lax.ppermute(send.reshape(batch, -1, send.shape[-1]), 'head', pairs)  17.9 us
    ppermute x6, starting transfers between devices, swap(): return lax.ppermute(send.reshape(batch, -1, send.shape[-1]), 'head', pairs)  7.78 us
    ppermute x2, starting transfers between devices, spread_out(): away_second = lax.ppermute(out, 'head', second_pairs)  4.61 us
    ppermute x2, waiting for transfers between devices, spread_out(): away_first = lax.ppermute(out, 'head', first_pairs)  3.8 us
    ppermute x2, waiting for transfers between devices, spread_out(): away_both = lax.ppermute(out, 'head', [(h, h ^ 6) for h in range(owners)])  3.34 us
  transfers between devices with their start and end apart: 26, of which 9 were waited for; matrix products, arithmetic and copies ran while one was open for 0% of the time, Pallas kernels for 43%

profile of v2, /device:TPU:0, one launch (start us, length us, event | category | flops | bytes accessed | tf_op | source)
XLA Modules:
  0.0 159.7 jit_solution(11215269347129268090)
XLA Ops:
  1.2 6.3 %shard_map.122 = (bf16[64,1920]{1,0:T(8,128)(2,1)}, bf16[64,1920]{1,0:T(8,128)(2,1)}, bf16[256,256]{1,0:T(8,128)(2,1)}) custom-call(s32[8,128]{1,0:T(8,128)} %bitcast.22, bf16[256,7168]{1,0:T(8,128)(2,1)} %refs_1_.1, bf16[56,128]{1,0:T(8,128)(2,1)} %bitcast.25, bf16[7168,128]{1,0:T(8,128)(2,1)} %refs_3_.2), custom_call_target="tpu_custom_call" | custom-call | flops 1 | bytes 1 | tf_op jit(solution)/shard_map/pallas_call | solution.py:33
  7.6 4.1 %collective-permute-start.3 = (bf16[64,1920]{1,0:T(8,128)(2,1)}, bf16[64,1920]{1,0:T(8,128)(2,1)}, u32[]{:S(2)}, u32[]{:S(2)}) collective-permute-start(bf16[64,1920]{1,0:T(8,128)(2,1)} %get-tuple-element.33.refs_0_), channel_id=1, source_target_pairs={{0,16},{8,24},{16,0},{24,8},{1,17},{9,25},{17,1},{25,9},{2,18},{10... | collective-permute-start | bytes 737288 | tf_op jit(solution)/shard_map/ppermute | solution.py:525
  11.7 1.6 collective-permute-start.2
  13.2 3.1 %collective-permute-done.refs_3_.refs_6_.refs_5_ = bf16[3,896,1792]{2,1,0:T(8,128)(2,1)} collective-permute-done((bf16[3,896,1792]{2,1,0:T(8,128)(2,1)}, bf16[3,896,1792]{2,1,0:T(8,128)(2,1)}, u32[]{:S(2)}, u32[]{:S(2)}) %collective-permute-start) | collective-permute-done | bytes 9633824 | tf_op jit(solution)/shard_map/ppermute | solution.py:527
  16.3 10.0 %shard_map.123 = (f32[64,5376]{1,0:T(8,128)}, bf16[64,5376]{1,0:T(8,128)(2,1)}) custom-call(bf16[64,1920]{1,0:T(8,128)(2,1)} %get-tuple-element.33.refs_0_, bf16[64,1920]{1,0:T(8,128)(2,1)} %get-tuple-element.34.refs_1_, bf16[3,896,1792]{2,1,0:T(8,128)(2,1)} %bitcast.27, bf16[3,896,1792]{2,1,0:T(8,128)(2,1)} %collective-permute-done.refs_3_.refs_6_.refs_5_, ...), custom_call_target="tpu_custom_call" | custom-call | flops 199999995904 | bytes 1 | tf_op jit(solution)/shard_map/pallas_call | solution.py:33
  27.3 3.0 %collective-permute-start.4 = (bf16[64,1920]{1,0:T(8,128)(2,1)S(1)}, bf16[64,1920]{1,0:T(8,128)(2,1)S(1)}, u32[]{:S(2)}, u32[]{:S(2)}) collective-permute-start(bf16[64,1920]{1,0:T(8,128)(2,1)S(1)} %shard_map.124), channel_id=1, source_target_pairs={{0,8},{8,0},{16,24},{24,16},{1,9},{9,1},{17,25},{25,17},{2,10},{10... | collective-permute-start | bytes 737288 | tf_op jit(solution)/shard_map/ppermute | solution.py:525
  30.3 1.5 collective-permute-start.5
  31.8 4.8 %collective-permute-done.4.refs_0_.refs_4_ = bf16[64,1920]{1,0:T(8,128)(2,1)S(1)} collective-permute-done((bf16[64,1920]{1,0:T(8,128)(2,1)S(1)}, bf16[64,1920]{1,0:T(8,128)(2,1)S(1)}, u32[]{:S(2)}, u32[]{:S(2)}) %collective-permute-start.4) | collective-permute-done | bytes 245792 | tf_op jit(solution)/shard_map/ppermute | solution.py:525
  37.3 2.7 %collective-permute-start.7 = (bf16[64,1920]{1,0:T(8,128)(2,1)}, bf16[64,1920]{1,0:T(8,128)(2,1)}, u32[]{:S(2)}, u32[]{:S(2)}) collective-permute-start(bf16[64,1920]{1,0:T(8,128)(2,1)} %shard_map.125.refs_1_), channel_id=1, source_target_pairs={{0,16},{8,24},{16,0},{24,8},{1,17},{9,25},{17,1},{25,9},{2,18},{10... | collective-permute-start | bytes 737288 | tf_op jit(solution)/shard_map/ppermute | solution.py:525
  40.1 1.6 collective-permute-start.6
  41.7 10.5 %shard_map.126 = (f32[96,5376]{1,0:T(8,128)}, bf16[96,5376]{1,0:T(8,128)(2,1)}) custom-call(bf16[64,5376]{1,0:T(8,128)(2,1)} %get-tuple-element.35.refs_0_, bf16[64,1920]{1,0:T(8,128)(2,1)} %shard_map.125.refs_1_, bf16[64,1920]{1,0:T(8,128)(2,1)} %collective-permute-done.2.refs_1_.refs_2_, bf16[64,1920]{1,0:T(8,128)(2,1)} %collective-permute-done.3.refs_2_.refs_3_, ...), custom_call_target="tpu_custom_call" | custom-call | flops 199999995904 | bytes 1 | tf_op jit(solution)/shard_map/pallas_call | solution.py:33
  54.1 1.5 collective-permute-start.9
  55.6 2.3 %shard_map.127 = (f32[2,16,5376]{2,1,0:T(8,128)S(1)}, bf16[2,16,5376]{2,1,0:T(8,128)(2,1)S(1)}) custom-call(bf16[96,5376]{1,0:T(8,128)(2,1)} %get-tuple-element.36.refs_0_, f32[2,32,5376]{2,1,0:T(8,128)S(1)} %bitcast.18, bf16[2,32,5376]{2,1,0:T(8,128)(2,1)} %collective-permute-done.5.refs_2_), custom_call_target="tpu_custom_call" | custom-call | flops 1 | bytes 1 | tf_op jit(solution)/shard_map/pallas_call | solution.py:33
  57.9 2.0 %shard_map.128 = (f32[2,64,64]{2,1,0:T(8,128)S(1)}, f32[2,8,64]{2,1,0:T(8,128)S(1)}) custom-call(bf16[2,16,5376]{2,1,0:T(8,128)(2,1)S(1)} %get-tuple-element.38.refs_0_, s32[8,128]{1,0:T(8,128)S(1)} %bitcast.23, s32[2,64]{1,0:T(2,128)S(1)} %copy-done.14, s32[2,8]{1,0:T(2,128)S(1)} %copy-done.15), custom_call_target="tpu_custom_call" | custom-call | flops 1 | bytes 1 | tf_op jit(solution)/shard_map/pallas_call | solution.py:33
  61.2 10.6 %shard_map.130 = (f32[96,5376]{1,0:T(8,128)}, bf16[96,5376]{1,0:T(8,128)(2,1)}) custom-call(f32[2,8,64]{2,1,0:T(8,128)} %copy-done.10, bf16[64,1920]{1,0:T(8,128)(2,1)} %collective-permute-done.6.refs_1_, bf16[64,1920]{1,0:T(8,128)(2,1)} %collective-permute-done.7.refs_2_, bf16[64,1920]{1,0:T(8,128)(2,1)} %copy-done.16, bf16[3,896,1792]{2,1,0:T(8,128)(2,1)} %bitcast.29, ...), custom_call_target="tpu_custom_call" | custom-call | flops 199999995904 | bytes 1 | tf_op jit(solution)/shard_map/pallas_call | solution.py:33
  74.2 2.4 %shard_map.131 = (f32[3,16,5376]{2,1,0:T(8,128)S(1)}, bf16[3,16,5376]{2,1,0:T(8,128)(2,1)S(1)}) custom-call(bf16[96,5376]{1,0:T(8,128)(2,1)S(1)} %copy-done.4, f32[3,32,5376]{2,1,0:T(8,128)S(1)} %bitcast.17, bf16[3,32,5376]{2,1,0:T(8,128)(2,1)} %collective-permute-done.9.refs_2_), custom_call_target="tpu_custom_call" | custom-call | flops 1 | bytes 1 | tf_op jit(solution)/shard_map/pallas_call | solution.py:33
  76.6 1.6 collective-permute-start.12
  78.7 17.8 %collective-permute-done.10.refs_2_ = bf16[3,32,5376]{2,1,0:T(8,128)(2,1)S(1)} collective-permute-done((bf16[3,32,5376]{2,1,0:T(8,128)(2,1)}, bf16[3,32,5376]{2,1,0:T(8,128)(2,1)S(1)}, u32[]{:S(2)}, u32[]{:S(2)}) %collective-permute-start.10) | collective-permute-done | bytes 1032224 | tf_op jit(solution)/shard_map/ppermute | solution.py:549
  97.2 1.6 %collective-permute-start.13 = (bf16[3,16,5376]{2,1,0:T(8,128)(2,1)S(1)}, bf16[3,16,5376]{2,1,0:T(8,128)(2,1)S(1)}, u32[]{:S(2)}, u32[]{:S(2)}) collective-permute-start(bf16[3,16,5376]{2,1,0:T(8,128)(2,1)S(1)} %get-tuple-element.44.refs_0_), channel_id=1, source_target_pairs={{0,4},{1,3},{2,6},{3,1},{4,0},{5,7},{6,2},{7,5},{8,12},{9,11},{10,... | collective-permute-start | bytes 1548296 | tf_op jit(solution)/shard_map/ppermute | solution.py:549
  99.2 11.1 %shard_map.134 = (bf16[64,1792]{1,0:T(8,128)(2,1)S(1)}, bf16[2,8,1792]{2,1,0:T(8,128)(2,1)S(1)}) custom-call(s32[2]{0:T(128)S(1)} %copy-done.13, bf16[64,5376]{1,0:T(8,128)(2,1)S(1)} %shard_map.133.refs_1_, f32[2,64,64]{2,1,0:T(8,128)S(1)} %get-tuple-element.47.refs_2_, f32[2,8,64]{2,1,0:T(8,128)S(1)} %copy-done.11, bf16[2,2,2048,1792]{3,2,1,0:T(8,128)(2,1)} %refs_4_.3), custom_call_target="tpu_custom_call" | custom-call | flops 1 | bytes 1 | tf_op jit(solution)/shard_map/pallas_call | solution.py:33
  110.6 3.2 %collective-permute-start.14 = (bf16[64,1792]{1,0:T(8,128)(2,1)S(1)}, bf16[64,1792]{1,0:T(8,128)(2,1)S(1)}, u32[]{:S(2)}, u32[]{:S(2)}) collective-permute-start(bf16[64,1792]{1,0:T(8,128)(2,1)S(1)} %get-tuple-element.48.refs_0_.refs_1_), channel_id=1, source_target_pairs={{0,4},{1,3},{2,6},{3,1},{4,0},{5,7},{6,2},{7,5},{8,12},{9,11},{10,... | collective-permute-start | bytes 688136 | tf_op jit(solution)/shard_map/ppermute | solution.py:600
  114.2 9.2 %shard_map.136 = (bf16[64,1792]{1,0:T(8,128)(2,1)S(1)}, bf16[2,8,1792]{2,1,0:T(8,128)(2,1)S(1)}) custom-call(s32[2]{0:T(128)S(1)} %copy-done.13, bf16[64,5376]{1,0:T(8,128)(2,1)S(1)} %shard_map.135.refs_1_, f32[2,64,64]{2,1,0:T(8,128)S(1)} %get-tuple-element.47.refs_2_, f32[2,8,64]{2,1,0:T(8,128)S(1)} %copy-done.11, bf16[2,2,2048,1792]{3,2,1,0:T(8,128)(2,1)} %refs_4_.3), custom_call_target="tpu_custom_call" | custom-call | flops 1 | bytes 1 | tf_op jit(solution)/shard_map/pallas_call | solution.py:33
  124.0 1.8 %collective-permute-start.19 = (bf16[64,1792]{1,0:T(8,128)(2,1)S(1)}, bf16[64,1792]{1,0:T(8,128)(2,1)S(1)}, u32[]{:S(2)}, u32[]{:S(2)}) collective-permute-start(bf16[64,1792]{1,0:T(8,128)(2,1)S(1)} %get-tuple-element.50.refs_0_.refs_1_), channel_id=1, source_target_pairs={{0,2},{1,5},{2,0},{3,7},{4,6},{5,1},{6,4},{7,3},{8,10},{9,13},{10,... | collective-permute-start | bytes 688136 | tf_op jit(solution)/shard_map/ppermute | solution.py:599
  125.8 1.4 collective-permute-start.18
  128.2 1.5 collective-permute-start.21
  129.7 3.3 %collective-permute-done.20.refs_4_ = bf16[64,1792]{1,0:T(8,128)(2,1)S(1)} collective-permute-done((bf16[64,1792]{1,0:T(8,128)(2,1)S(1)}, bf16[64,1792]{1,0:T(8,128)(2,1)S(1)}, u32[]{:S(2)}, u32[]{:S(2)}) %collective-permute-start.20) | collective-permute-done | bytes 229408 | tf_op jit(solution)/shard_map/ppermute | solution.py:601
  133.0 3.8 %collective-permute-done.19.refs_3_ = bf16[64,1792]{1,0:T(8,128)(2,1)S(1)} collective-permute-done((bf16[64,1792]{1,0:T(8,128)(2,1)S(1)}, bf16[64,1792]{1,0:T(8,128)(2,1)S(1)}, u32[]{:S(2)}, u32[]{:S(2)}) %collective-permute-start.19) | collective-permute-done | bytes 229408 | tf_op jit(solution)/shard_map/ppermute | solution.py:599
  137.7 2.5 %collective-permute-done.23.refs_1_ = bf16[256,1792]{1,0:T(8,128)(2,1)S(1)} collective-permute-done((bf16[256,1792]{1,0:T(8,128)(2,1)S(1)}, bf16[256,1792]{1,0:T(8,128)(2,1)S(1)}, u32[]{:S(2)}, u32[]{:S(2)}) %collective-permute-start.23) | collective-permute-done | bytes 917536 | tf_op jit(solution)/shard_map/ppermute | solution.py:610
  141.2 1.5 collective-permute-start.24
  142.6 1.4 collective-permute-start.22
  144.1 7.2 %collective-permute-done.24.refs_1_ = bf16[2,448,128]{2,1,0:T(8,128)(2,1)S(1)} collective-permute-done((bf16[2,448,128]{2,1,0:T(8,128)(2,1)S(1)}, bf16[2,448,128]{2,1,0:T(8,128)(2,1)S(1)}, u32[]{:S(2)}, u32[]{:S(2)}) %collective-permute-start.24) | collective-permute-done | bytes 229408 | tf_op jit(solution)/shard_map/ppermute | solution.py:525
  152.5 6.3 %collective-permute-done.25.refs_4_ = bf16[448,128]{1,0:T(8,128)(2,1)S(1)} collective-permute-done((bf16[448,128]{1,0:T(8,128)(2,1)S(1)}, bf16[448,128]{1,0:T(8,128)(2,1)S(1)}, u32[]{:S(2)}, u32[]{:S(2)}) %collective-permute-start.25) | collective-permute-done | bytes 114720 | tf_op jit(solution)/shard_map/ppermute | solution.py:525
  (80 shorter events, 15.6 us)
Async XLA Ops:
  0.6 15.7 %collective-permute-start = (bf16[3,896,1792]{2,1,0:T(8,128)(2,1)}, bf16[3,896,1792]{2,1,0:T(8,128)(2,1)}, u32[]{:S(2)}, u32[]{:S(2)}) collective-permute-start(bf16[3,896,1792]{2,1,0:T(8,128)(2,1)} %bitcast.26), channel_id=1, source_target_pairs={{0,1},{1,0},{2,3},{3,2},{4,5},{5,4},{6,7},{7,6},{8,9},{9,8},{10,11... | collective-permute-start | bytes 28901384 | tf_op jit(solution)/shard_map/ppermute | solution.py:527
  1.1 12.1 %collective-permute-start.1 = (bf16[3,16,1792]{2,1,0:T(8,128)(2,1)}, bf16[3,16,1792]{2,1,0:T(8,128)(2,1)S(1)}, u32[]{:S(2)}, u32[]{:S(2)}) collective-permute-start(bf16[3,16,1792]{2,1,0:T(8,128)(2,1)} %bitcast.30), channel_id=1, source_target_pairs={{0,1},{1,0},{2,3},{3,2},{4,5},{5,4},{6,7},{7,6},{8,9},{9,8},{10,11... | collective-permute-start | bytes 516104 | tf_op jit(solution)/shard_map/ppermute | solution.py:528
  7.6 18.7 %collective-permute-start.3 = (bf16[64,1920]{1,0:T(8,128)(2,1)}, bf16[64,1920]{1,0:T(8,128)(2,1)}, u32[]{:S(2)}, u32[]{:S(2)}) collective-permute-start(bf16[64,1920]{1,0:T(8,128)(2,1)} %get-tuple-element.33.refs_0_), channel_id=1, source_target_pairs={{0,16},{8,24},{16,0},{24,8},{1,17},{9,25},{17,1},{25,9},{2,18},{10... | collective-permute-start | bytes 737288 | tf_op jit(solution)/shard_map/ppermute | solution.py:525
  11.7 14.6 %collective-permute-start.2 = (bf16[64,1920]{1,0:T(8,128)(2,1)}, bf16[64,1920]{1,0:T(8,128)(2,1)}, u32[]{:S(2)}, u32[]{:S(2)}) collective-permute-start(bf16[64,1920]{1,0:T(8,128)(2,1)} %get-tuple-element.33.refs_0_), channel_id=1, source_target_pairs={{0,8},{8,0},{16,24},{24,16},{1,9},{9,1},{17,25},{25,17},{2,10},{10... | collective-permute-start | bytes 737288 | tf_op jit(solution)/shard_map/ppermute | solution.py:525
  16.3 20.2 %copy-start.7 = (bf16[64,1920]{1,0:T(8,128)(2,1)S(1)}, bf16[64,1920]{1,0:T(8,128)(2,1)}, u32[]{:S(2)}) copy-start(bf16[64,1920]{1,0:T(8,128)(2,1)} %get-tuple-element.34.refs_1_) | copy-start | bytes 737284
  27.3 9.3 %collective-permute-start.4 = (bf16[64,1920]{1,0:T(8,128)(2,1)S(1)}, bf16[64,1920]{1,0:T(8,128)(2,1)S(1)}, u32[]{:S(2)}, u32[]{:S(2)}) collective-permute-start(bf16[64,1920]{1,0:T(8,128)(2,1)S(1)} %shard_map.124), channel_id=1, source_target_pairs={{0,8},{8,0},{16,24},{24,16},{1,9},{9,1},{17,25},{25,17},{2,10},{10... | collective-permute-start | bytes 737288 | tf_op jit(solution)/shard_map/ppermute | solution.py:525
  30.3 25.3 %collective-permute-start.5 = (bf16[2,32,5376]{2,1,0:T(8,128)(2,1)}, bf16[2,32,5376]{2,1,0:T(8,128)(2,1)}, u32[]{:S(2)}, u32[]{:S(2)}) collective-permute-start(bf16[2,32,5376]{2,1,0:T(8,128)(2,1)} %bitcast.5), channel_id=1, source_target_pairs={{0,2},{1,5},{2,0},{3,7},{4,6},{5,1},{6,4},{7,3},{8,10},{9,13},{10,... | collective-permute-start | bytes 2064392 | tf_op jit(solution)/shard_map/ppermute | solution.py:549
  37.3 14.8 %collective-permute-start.7 = (bf16[64,1920]{1,0:T(8,128)(2,1)}, bf16[64,1920]{1,0:T(8,128)(2,1)}, u32[]{:S(2)}, u32[]{:S(2)}) collective-permute-start(bf16[64,1920]{1,0:T(8,128)(2,1)} %shard_map.125.refs_1_), channel_id=1, source_target_pairs={{0,16},{8,24},{16,0},{24,8},{1,17},{9,25},{17,1},{25,9},{2,18},{10... | collective-permute-start | bytes 737288 | tf_op jit(solution)/shard_map/ppermute | solution.py:525
  40.1 12.1 %collective-permute-start.6 = (bf16[64,1920]{1,0:T(8,128)(2,1)}, bf16[64,1920]{1,0:T(8,128)(2,1)}, u32[]{:S(2)}, u32[]{:S(2)}) collective-permute-start(bf16[64,1920]{1,0:T(8,128)(2,1)} %shard_map.125.refs_1_), channel_id=1, source_target_pairs={{0,8},{8,0},{16,24},{24,16},{1,9},{9,1},{17,25},{25,17},{2,10},{10... | collective-permute-start | bytes 737288 | tf_op jit(solution)/shard_map/ppermute | solution.py:525
  52.2 5.7 %copy-start.12 = (s32[1024]{0:T(1024)S(1)}, s32[1024]{0:T(1024)}, u32[]{:S(2)}) copy-start(s32[1024]{0:T(1024)} %param.12) | copy-start | bytes 12292
  52.2 5.7 %copy-start.14 = (s32[2,64]{1,0:T(2,128)S(1)}, s32[2,64]{1,0:T(2,128)}, u32[]{:S(2)}) copy-start(s32[2,64]{1,0:T(2,128)} %refs_2_.1) | copy-start | bytes 1540
  53.3 7.2 %collective-permute-start.8 = (bf16[64,1920]{1,0:T(8,128)(2,1)S(1)}, bf16[64,1920]{1,0:T(8,128)(2,1)S(1)}, u32[]{:S(2)}, u32[]{:S(2)}) collective-permute-start(bf16[64,1920]{1,0:T(8,128)(2,1)S(1)} %shard_map.129), channel_id=1, source_target_pairs={{0,8},{8,0},{16,24},{24,16},{1,9},{9,1},{17,25},{25,17},{2,10},{10... | collective-permute-start | bytes 737288 | tf_op jit(solution)/shard_map/ppermute | solution.py:525
  54.1 18.9 %collective-permute-start.9 = (bf16[3,32,5376]{2,1,0:T(8,128)(2,1)}, bf16[3,32,5376]{2,1,0:T(8,128)(2,1)}, u32[]{:S(2)}, u32[]{:S(2)}) collective-permute-start(bf16[3,32,5376]{2,1,0:T(8,128)(2,1)} %bitcast.7), channel_id=1, source_target_pairs={{0,2},{1,5},{2,0},{3,7},{4,6},{5,1},{6,4},{7,3},{8,10},{9,13},{10,... | collective-permute-start | bytes 3096584 | tf_op jit(solution)/shard_map/ppermute | solution.py:549
  61.2 11.7 %copy-start.2 = (f32[96,5376]{1,0:T(8,128)S(1)}, f32[96,5376]{1,0:T(8,128)}, u32[]{:S(2)}) copy-start(f32[96,5376]{1,0:T(8,128)} %get-tuple-element.41) | copy-start | bytes 6193156
  71.9 24.7 %collective-permute-start.10 = (bf16[3,32,5376]{2,1,0:T(8,128)(2,1)}, bf16[3,32,5376]{2,1,0:T(8,128)(2,1)S(1)}, u32[]{:S(2)}, u32[]{:S(2)}) collective-permute-start(bf16[3,32,5376]{2,1,0:T(8,128)(2,1)} %bitcast.19), channel_id=1, source_target_pairs={{0,2},{1,5},{2,0},{3,7},{4,6},{5,1},{6,4},{7,3},{8,10},{9,13},{10,... | collective-permute-start | bytes 3096584 | tf_op jit(solution)/shard_map/ppermute | solution.py:549
  74.2 22.4 %copy-start.1 = (f32[96,5376]{1,0:T(8,128)S(1)}, f32[96,5376]{1,0:T(8,128)}, u32[]{:S(2)}) copy-start(f32[96,5376]{1,0:T(8,128)} %get-tuple-element.43) | copy-start | bytes 6193156
  76.6 22.1 %collective-permute-start.12 = (bf16[3,16,5376]{2,1,0:T(8,128)(2,1)S(1)}, bf16[3,16,5376]{2,1,0:T(8,128)(2,1)S(1)}, u32[]{:S(2)}, u32[]{:S(2)}) collective-permute-start(bf16[3,16,5376]{2,1,0:T(8,128)(2,1)S(1)} %get-tuple-element.42.refs_0_), channel_id=1, source_target_pairs={{0,4},{1,3},{2,6},{3,1},{4,0},{5,7},{6,2},{7,5},{8,12},{9,11},{10,... | collective-permute-start | bytes 1548296 | tf_op jit(solution)/shard_map/ppermute | solution.py:549
  78.2 20.6 %collective-permute-start.11 = (bf16[2,16,5376]{2,1,0:T(8,128)(2,1)S(1)}, bf16[2,16,5376]{2,1,0:T(8,128)(2,1)S(1)}, u32[]{:S(2)}, u32[]{:S(2)}) collective-permute-start(bf16[2,16,5376]{2,1,0:T(8,128)(2,1)S(1)} %copy-done.6), channel_id=1, source_target_pairs={{0,4},{1,3},{2,6},{3,1},{4,0},{5,7},{6,2},{7,5},{8,12},{9,11},{10,... | collective-permute-start | bytes 1032200 | tf_op jit(solution)/shard_map/ppermute | solution.py:549
  97.2 16.7 %collective-permute-start.13 = (bf16[3,16,5376]{2,1,0:T(8,128)(2,1)S(1)}, bf16[3,16,5376]{2,1,0:T(8,128)(2,1)S(1)}, u32[]{:S(2)}, u32[]{:S(2)}) collective-permute-start(bf16[3,16,5376]{2,1,0:T(8,128)(2,1)S(1)} %get-tuple-element.44.refs_0_), channel_id=1, source_target_pairs={{0,4},{1,3},{2,6},{3,1},{4,0},{5,7},{6,2},{7,5},{8,12},{9,11},{10,... | collective-permute-start | bytes 1548296 | tf_op jit(solution)/shard_map/ppermute | solution.py:549
  110.3 13.2 %collective-permute-start.16 = (bf16[64,1792]{1,0:T(8,128)(2,1)S(1)}, bf16[64,1792]{1,0:T(8,128)(2,1)S(1)}, u32[]{:S(2)}, u32[]{:S(2)}) collective-permute-start(bf16[64,1792]{1,0:T(8,128)(2,1)S(1)} %get-tuple-element.48.refs_0_.refs_1_), channel_id=1, source_target_pairs={{0,6},{1,7},{2,4},{3,5},{4,2},{5,3},{6,0},{7,1},{8,14},{9,15},{10,... | collective-permute-start | bytes 688136 | tf_op jit(solution)/shard_map/ppermute | solution.py:601
  110.6 12.8 %collective-permute-start.15 = (bf16[64,1792]{1,0:T(8,128)(2,1)S(1)}, bf16[64,1792]{1,0:T(8,128)(2,1)S(1)}, u32[]{:S(2)}, u32[]{:S(2)}) collective-permute-start(bf16[64,1792]{1,0:T(8,128)(2,1)S(1)} %get-tuple-element.48.refs_0_.refs_1_), channel_id=1, source_target_pairs={{0,2},{1,5},{2,0},{3,7},{4,6},{5,1},{6,4},{7,3},{8,10},{9,13},{10,... | collective-permute-start | bytes 688136 | tf_op jit(solution)/shard_map/ppermute | solution.py:599
  110.6 12.8 %collective-permute-start.14 = (bf16[64,1792]{1,0:T(8,128)(2,1)S(1)}, bf16[64,1792]{1,0:T(8,128)(2,1)S(1)}, u32[]{:S(2)}, u32[]{:S(2)}) collective-permute-start(bf16[64,1792]{1,0:T(8,128)(2,1)S(1)} %get-tuple-element.48.refs_0_.refs_1_), channel_id=1, source_target_pairs={{0,4},{1,3},{2,6},{3,1},{4,0},{5,7},{6,2},{7,5},{8,12},{9,11},{10,... | collective-permute-start | bytes 688136 | tf_op jit(solution)/shard_map/ppermute | solution.py:600
  123.5 3.6 %collective-permute-start.17 = (bf16[256,1792]{1,0:T(8,128)(2,1)S(1)}, bf16[256,1792]{1,0:T(8,128)(2,1)S(1)}, u32[]{:S(2)}, u32[]{:S(2)}) collective-permute-start(bf16[256,1792]{1,0:T(8,128)(2,1)S(1)} %shard_map.137.refs_0_), channel_id=1, source_target_pairs={{0,1},{1,0},{2,3},{3,2},{4,5},{5,4},{6,7},{7,6},{8,9},{9,8},{10,11... | collective-permute-start | bytes 2752520 | tf_op jit(solution)/shard_map/ppermute | solution.py:610
  123.6 9.4 %collective-permute-start.20 = (bf16[64,1792]{1,0:T(8,128)(2,1)S(1)}, bf16[64,1792]{1,0:T(8,128)(2,1)S(1)}, u32[]{:S(2)}, u32[]{:S(2)}) collective-permute-start(bf16[64,1792]{1,0:T(8,128)(2,1)S(1)} %get-tuple-element.50.refs_0_.refs_1_), channel_id=1, source_target_pairs={{0,6},{1,7},{2,4},{3,5},{4,2},{5,3},{6,0},{7,1},{8,14},{9,15},{10,... | collective-permute-start | bytes 688136 | tf_op jit(solution)/shard_map/ppermute | solution.py:601
  124.0 12.9 %collective-permute-start.19 = (bf16[64,1792]{1,0:T(8,128)(2,1)S(1)}, bf16[64,1792]{1,0:T(8,128)(2,1)S(1)}, u32[]{:S(2)}, u32[]{:S(2)}) collective-permute-start(bf16[64,1792]{1,0:T(8,128)(2,1)S(1)} %get-tuple-element.50.refs_0_.refs_1_), channel_id=1, source_target_pairs={{0,2},{1,5},{2,0},{3,7},{4,6},{5,1},{6,4},{7,3},{8,10},{9,13},{10,... | collective-permute-start | bytes 688136 | tf_op jit(solution)/shard_map/ppermute | solution.py:599
  125.8 11.7 %collective-permute-start.18 = (bf16[64,1792]{1,0:T(8,128)(2,1)S(1)}, bf16[64,1792]{1,0:T(8,128)(2,1)S(1)}, u32[]{:S(2)}, u32[]{:S(2)}) collective-permute-start(bf16[64,1792]{1,0:T(8,128)(2,1)S(1)} %get-tuple-element.50.refs_0_.refs_1_), channel_id=1, source_target_pairs={{0,4},{1,3},{2,6},{3,1},{4,0},{5,7},{6,2},{7,5},{8,12},{9,11},{10,... | collective-permute-start | bytes 688136 | tf_op jit(solution)/shard_map/ppermute | solution.py:600
  128.2 9.3 %collective-permute-start.21 = (bf16[2,448,128]{2,1,0:T(8,128)(2,1)S(1)}, bf16[2,448,128]{2,1,0:T(8,128)(2,1)S(1)}, u32[]{:S(2)}, u32[]{:S(2)}) collective-permute-start(bf16[2,448,128]{2,1,0:T(8,128)(2,1)S(1)} %get-tuple-element.52), channel_id=1, source_target_pairs={{0,8},{8,0},{16,24},{24,16},{1,9},{9,1},{17,25},{25,17},{2,10},{10... | collective-permute-start | bytes 688136 | tf_op jit(solution)/shard_map/ppermute | solution.py:525
  137.6 21.2 %copy-start.9 = (bf16[256,256]{1,0:T(8,128)(2,1)S(1)}, bf16[256,256]{1,0:T(8,128)(2,1)}, u32[]{:S(2)}) copy-start(bf16[256,256]{1,0:T(8,128)(2,1)} %get-tuple-element.32.refs_0_) | copy-start | bytes 393220
  137.6 2.5 %collective-permute-start.23 = (bf16[256,1792]{1,0:T(8,128)(2,1)S(1)}, bf16[256,1792]{1,0:T(8,128)(2,1)S(1)}, u32[]{:S(2)}, u32[]{:S(2)}) collective-permute-start(bf16[256,1792]{1,0:T(8,128)(2,1)S(1)} %get-tuple-element.55.refs_0_), channel_id=1, source_target_pairs={{0,1},{1,0},{2,3},{3,2},{4,5},{5,4},{6,7},{7,6},{8,9},{9,8},{10,11... | collective-permute-start | bytes 2752520 | tf_op jit(solution)/shard_map/ppermute | solution.py:610
  141.2 10.2 %collective-permute-start.24 = (bf16[2,448,128]{2,1,0:T(8,128)(2,1)S(1)}, bf16[2,448,128]{2,1,0:T(8,128)(2,1)S(1)}, u32[]{:S(2)}, u32[]{:S(2)}) collective-permute-start(bf16[2,448,128]{2,1,0:T(8,128)(2,1)S(1)} %get-tuple-element.57), channel_id=1, source_target_pairs={{0,8},{8,0},{16,24},{24,16},{1,9},{9,1},{17,25},{25,17},{2,10},{10... | collective-permute-start | bytes 688136 | tf_op jit(solution)/shard_map/ppermute | solution.py:525
  142.6 9.8 %collective-permute-start.22 = (bf16[448,128]{1,0:T(8,128)(2,1)S(1)}, bf16[448,128]{1,0:T(8,128)(2,1)S(1)}, u32[]{:S(2)}, u32[]{:S(2)}) collective-permute-start(bf16[448,128]{1,0:T(8,128)(2,1)S(1)} %get-tuple-element.54), channel_id=1, source_target_pairs={{0,16},{8,24},{16,0},{24,8},{1,17},{9,25},{17,1},{25,9},{2,18},{10... | collective-permute-start | bytes 344072 | tf_op jit(solution)/shard_map/ppermute | solution.py:525
  151.4 7.4 %collective-permute-start.25 = (bf16[448,128]{1,0:T(8,128)(2,1)S(1)}, bf16[448,128]{1,0:T(8,128)(2,1)S(1)}, u32[]{:S(2)}, u32[]{:S(2)}) collective-permute-start(bf16[448,128]{1,0:T(8,128)(2,1)S(1)} %get-tuple-element.59), channel_id=1, source_target_pairs={{0,16},{8,24},{16,0},{24,8},{1,17},{9,25},{17,1},{25,9},{2,18},{10... | collective-permute-start | bytes 344072 | tf_op jit(solution)/shard_map/ppermute | solution.py:525
  (12 other events, 34.4 us)

commit v3 on v2

--- a/solution.py
+++ b/solution.py
@@ -61,7 +61,7 @@
 CHUNK = 32
 
 
-def norm_kernel(slots, rank_rows, ids_ref, stream_hbm, gain_ref, down_hbm, first_ref, second_ref,
+def norm_kernel(slots, rank_rows, ids_ref, stream_hbm, gain_ref, down_hbm, feature_ref,
                 place_ref, normed, held, down_ref, arrived, down_arrived):
     me = lax.axis_index("head")
     plane = lax.axis_index("tok")
@@ -115,15 +115,11 @@
     quarter = half // 2
     position = jnp.where(order < 4, second * quarter + order * slots + rank % slots, -1)
     place = (lax.broadcasted_iota(jnp.int32, (half, rows), 0) == position).astype(BF16)
-    columns = (first_ref.shape[1] - LANES) // 2
+    columns = (feature_ref.shape[1] - LANES) // 2
     for i, owner_of in enumerate((me, me ^ 1)):
         block = normed[:, pl.ds(pl.multiple_of(owner_of * columns, LANES), columns)]
-        sorted_block = dot(place, block).astype(BF16)
-        first_ref[:, i * columns : (i + 1) * columns] = sorted_block[:quarter]
-        second_ref[:, i * columns : (i + 1) * columns] = sorted_block[quarter:]
-    sorted_low = dot(place, low).astype(BF16)
-    first_ref[:, 2 * columns :] = sorted_low[:quarter]
-    second_ref[:, 2 * columns :] = sorted_low[quarter:]
+        feature_ref[:, i * columns : (i + 1) * columns] = dot(place, block).astype(BF16)
+    feature_ref[:, 2 * columns :] = dot(place, low).astype(BF16)
 
 
 def prep_kernel(slots, planes, rows, ids_ref, parents_ref, accepted_ref, mask_ref, chosen_ref):
@@ -184,10 +180,13 @@
             inward(i, side).start()
     at = 0
     for lhs_ref in lhs_refs:
-        rows = lhs_ref.shape[0] // 2
-        lhs[at : at + rows, :] = lhs_ref[:rows, :]
-        lhs[half + at : half + at + rows, :] = lhs_ref[rows:, :]
-        at += rows
+        rows = lhs_ref.shape[0] // 4
+        for j in range(2):
+            lhs[at : at + rows, :] = lhs_ref[2 * j * rows : (2 * j + 1) * rows, :]
+            lhs[half + at : half + at + rows, :] = lhs_ref[
+                (2 * j + 1) * rows : (2 * j + 2) * rows, :
+            ]
+            at += rows
     for p in range(parts):
         low = 2 * columns
         for side in range(2):
@@ -221,7 +220,7 @@
         after,
         (*pieces, *weights, *ups),
         [whole(piece.shape) for piece in pieces] + [far] * 2 + [whole(ups[0].shape)] * 2,
-        58,
+        55,
         LARGE,
         out_specs=[far] * 2,
         out_shape=[
@@ -269,29 +268,53 @@
     )
 
 
-def join_kernel(own_keep_ref, own_got_ref, keep_ref, got_ref, out_ref):
-    slots = own_keep_ref.shape[0]
-    out_ref[:slots] = (own_keep_ref[...] + own_got_ref[...].astype(F32)).astype(BF16)
-    for k in range(keep_ref.shape[0]):
-        out_ref[(k + 1) * slots : (k + 2) * slots] = (
-            keep_ref[k] + got_ref[k].astype(F32)
-        ).astype(BF16)
-
-
-def join(j, own, rest, parts, after=()):
-    batch, slots, wide = rest[0].shape
+def pass_kernel(*refs):
+    pass
+
+
+def pass_on(array, after):
+    return ordered(
+        pass_kernel,
+        (*after, array),
+        (),
+        [],
+        16,
+        out_specs=pl.BlockSpec(memory_space=pl.ANY),
+        out_shape=jax.ShapeDtypeStruct(array.shape, array.dtype),
+        input_output_aliases={len(after): 0},
+    )
+
+
+def join_kernel(*refs):
+    out_ref = refs[-1]
+    slots = refs[0].shape[-2]
+    at = 0
+    for keep_ref, got_ref in zip(refs[:-1:2], refs[1:-1:2]):
+        for k in range(keep_ref.shape[0]):
+            out_ref[at : at + slots] = (keep_ref[k] + got_ref[k].astype(F32)).astype(BF16)
+            at += slots
+
+
+def join(j, pairs, parts, after=()):
+    slots, wide = pairs[0][0].shape[1:]
     tile = wide // parts
-    near = pl.BlockSpec((None, slots, tile), lambda c: (j, 0, c))
-    far = pl.BlockSpec((batch, slots, tile), lambda c: (0, 0, c))
+    specs = []
+    operands = []
+    for pair in pairs:
+        planes = pair[0].shape[0] // 2
+        spec = pl.BlockSpec((planes, None, slots, tile), lambda c: (0, j, 0, c))
+        specs += [spec, spec]
+        operands += [array.reshape(planes, 2, slots, wide) for array in pair]
+    rows = sum(pair[0].shape[0] for pair in pairs) // 2 * slots
     return ordered(
         join_kernel,
         after,
-        (*own, *rest),
-        [near, near, far, far],
+        operands,
+        specs,
         16,
         grid=(parts,),
-        out_specs=pl.BlockSpec(((batch + 1) * slots, tile), lambda c: (0, c)),
-        out_shape=jax.ShapeDtypeStruct(((batch + 1) * slots, wide), BF16),
+        out_specs=pl.BlockSpec((rows, tile), lambda c: (0, c)),
+        out_shape=jax.ShapeDtypeStruct((rows, wide), BF16),
     )
 
 
@@ -526,15 +549,17 @@
 
     weights = (weight, lax.ppermute(weight, "head", core_pairs))
     ups = (up, lax.ppermute(up, "head", core_pairs))
-    feature = jax.ShapeDtypeStruct((rows // 4, 2 * columns + LANES), BF16)
-    first, second, place = ordered(
+    feature, place = ordered(
         functools.partial(norm_kernel, slots, rank_rows),
         (),
         (ids, stream, input_norm_gain.reshape(-1, LANES), adapter_down_weight),
         [whole(ids.shape), pl.BlockSpec(memory_space=pltpu.HBM),
          whole((width_in // LANES, LANES)), pl.BlockSpec(memory_space=pltpu.HBM)],
-        58,
-        out_shape=[feature, feature, jax.ShapeDtypeStruct((rows, rows), BF16)],
+        62,
+        out_shape=[
+            jax.ShapeDtypeStruct((rows // 2, 2 * columns + LANES), BF16),
+            jax.ShapeDtypeStruct((rows, rows), BF16),
+        ],
         scratch_shapes=[
             pltpu.VMEM((rows, width_in), BF16),
             pltpu.VMEM((rows, width_in), BF16),
@@ -543,36 +568,16 @@
             pltpu.SemaphoreType.DMA,
         ],
     )
-    near = [first, second]
 
     def swap(send, pairs, batch):
         return lax.ppermute(send.reshape(batch, -1, send.shape[-1]), "head", pairs)
 
-    def split(keep, got, batch, after):
+    def split(keep, got, batch, after=()):
         return halve(keep.reshape(batch, -1, keep.shape[-1]), got, 3, after)
 
-    rest = planes - 1
-
-    def relay(piece, after):
-        return ordered(
-            pack_kernel,
-            after,
-            (piece,),
-            [whole(piece.shape)],
-            16,
-            out_shape=jax.ShapeDtypeStruct(piece.shape, BF16),
-        )
-
-    beside, beyond = across(first, 1), across(first, 2)
-    own_keep, own_send = project(near, weights, ups)
-    far0 = [beside, beyond, across(relay(beyond, (own_send, beside)), 1)]
-    later = relay(second, (far0[2],))
-    beside, beyond = across(later, 1), across(later, 2)
+    beyond, beside = across(feature, 2), across(feature, 1)
+    own_keep, own_send = project([feature], weights, ups)
     own_got = swap(own_send, first_pairs, 2)
-    keep0, send0 = project(far0, weights, ups, (own_send, later))
-    got0 = swap(send0, first_pairs, rest)
-    own_keep, own_send = split(own_keep, own_got, 2, (send0,))
-    own_got = swap(own_send, second_pairs, 2)
     depth = accepted.shape[1]
     masks, chosen = ordered(
         functools.partial(prep_kernel, slots, planes, rows),
@@ -585,14 +590,20 @@
             jax.ShapeDtypeStruct((2, depth, NODES), F32),
         ],
     )
-    far1 = [beside, beyond, across(relay(beyond, (send0, beside)), 1)]
-    keep1, send1 = project(far1, weights, ups, (chosen,))
-    got1 = swap(send1, first_pairs, rest)
-    keep0, send0 = split(keep0, got0, rest, (send1,))
-    got0 = swap(send0, second_pairs, rest)
-    keep1, send1 = split(keep1, got1, rest, (send0,))
-    got1 = swap(send1, second_pairs, rest)
-    triple = join(0, (own_keep, own_got), (keep0, got0), 3, (send1,))
+    onward = pass_on(beyond, (chosen, beside))
+    furthest = across(onward, 1)
+    mid_keep, mid_send = project([beside, onward], weights, ups)
+    mid_got = swap(mid_send, first_pairs, 4)
+    own_keep, own_send = split(own_keep, own_got, 2, (mid_send,))
+    own_got = swap(own_send, second_pairs, 2)
+    far_keep, far_send = project([furthest], weights, ups, (own_send,))
+    far_got = swap(far_send, first_pairs, 2)
+    mid_keep, mid_send = split(mid_keep, mid_got, 4, (far_send,))
+    mid_got = swap(mid_send, second_pairs, 4)
+    far_keep, far_send = split(far_keep, far_got, 2, (mid_send,))
+    far_got = swap(far_send, second_pairs, 2)
+    pairs = ((own_keep, own_got), (mid_keep, mid_got), (far_keep, far_got))
+    triple = join(0, pairs, 3)
     out0, kept0 = attend(0, cache_length, triple, masks, chosen, key_value_cache)
 
     def spread_out(out):
@@ -602,7 +613,7 @@
         return (out, away_second, away_first, away_both)
 
     side0 = spread_out(out0)
-    triple = join(1, (own_keep, own_got), (keep1, got1), 3, (out0,))
+    triple = join(1, pairs, 3, (out0,))
     out1, kept1 = attend(1, cache_length, triple, masks, chosen, key_value_cache)
     side1 = spread_out(out1)
 

time: 160 us -> 154 us (0.963)
  starting transfers between devices: 34.3 us -> 27.2 us
  local copies, waits for them, and re-layouts: 3.28 us -> 5.96 us
  Pallas kernels: 71.7 us -> 69.7 us
    ppermute x10 -> x7, starting transfers between devices: 18.6 us -> 11 us  [across(): return lax.ppermute(array, 'tok', [(z, z ^ k) for z in range(planes)])]
    unnamed x37 -> x33, local copies, waits for them, and re-layouts: 3.28 us -> 5.96 us
    ppermute x2, starting transfers between devices: 1.79 us -> 4.34 us  [spread_out(): away_first = lax.ppermute(out, 'head', first_pairs)]
    ppermute x6, waiting for transfers between devices: 17.9 us -> 15.5 us  [swap(): return lax.ppermute(send.reshape(batch, -1, send.shape[-1]), 'head', pairs)]
    ppermute x2, starting transfers between devices: 4.61 us -> 2.55 us  [spread_out(): away_second = lax.ppermute(out, 'head', second_pairs)]
    pallas_call x22 -> x20, Pallas kernels: 71.7 us -> 69.7 us  [ordered(): pl.pallas_call(body, in_specs=[pl.BlockSpec(memory_space=pl.ANY)] * count...]
    ppermute x10 -> x7, waiting for transfers between devices: 18.4 us -> 19.7 us  [across(): return lax.ppermute(array, 'tok', [(z, z ^ k) for z in range(planes)])]
  transfers between devices with their start and end apart: 26 -> 23, of which waited for: 9 -> 12; matrix products, arithmetic and copies ran while one was open for 0% -> 0% of each run, Pallas kernels for 43% -> 37%
where the time goes in v3:
time: 154 us
  Pallas kernels  69.7 us (45%)
  waiting for transfers between devices  50 us (32%)
  starting transfers between devices  27.2 us (18%)
  local copies, waits for them, and re-layouts  5.96 us (4%)
    pallas_call x20, Pallas kernels, ordered(): pl.pallas_call(body, in_specs=[pl.BlockSpec(memory_space=pl.ANY)] * count...  69.7 us
    ppermute x7, waiting for transfers between devices, across(): return lax.ppermute(array, 'tok', [(z, z ^ k) for z in range(planes)])  19.7 us
    ppermute x6, waiting for transfers between devices, swap(): return lax.ppermute(send.reshape(batch, -1, send.shape[-1]), 'head', pairs)  15.5 us
    ppermute x7, starting transfers between devices, across(): return lax.ppermute(array, 'tok', [(z, z ^ k) for z in range(planes)])  11 us
    ppermute x6, starting transfers between devices, swap(): return lax.ppermute(send.reshape(batch, -1, send.shape[-1]), 'head', pairs)  8.36 us
    unnamed x33, local copies, waits for them, and re-layouts  5.96 us
    ppermute x2, waiting for transfers between devices, spread_out(): away_first = lax.ppermute(out, 'head', first_pairs)  4.98 us
    ppermute x2, starting transfers between devices, spread_out(): away_first = lax.ppermute(out, 'head', first_pairs)  4.34 us
  transfers between devices with their start and end apart: 23, of which 12 were waited for; matrix products, arithmetic and copies ran while one was open for 0% of the time, Pallas kernels for 37%

profile of v3, /device:TPU:0, one launch (start us, length us, event | category | flops | bytes accessed | tf_op | source)
XLA Modules:
  0.0 153.7 jit_solution(14297017402740870780)
XLA Ops:
  1.2 6.3 %shard_map.122 = (bf16[128,1920]{1,0:T(8,128)(2,1)}, bf16[256,256]{1,0:T(8,128)(2,1)}) custom-call(s32[8,128]{1,0:T(8,128)} %bitcast.41, bf16[256,7168]{1,0:T(8,128)(2,1)} %refs_1_.1, bf16[56,128]{1,0:T(8,128)(2,1)} %bitcast.44, bf16[7168,128]{1,0:T(8,128)(2,1)} %refs_3_.2), custom_call_target="tpu_custom_call" | custom-call | flops 1 | bytes 1 | tf_op jit(solution)/shard_map/pallas_call | solution.py:33
  7.6 4.1 %collective-permute-start.3 = (bf16[128,1920]{1,0:T(8,128)(2,1)}, bf16[128,1920]{1,0:T(8,128)(2,1)}, u32[]{:S(2)}, u32[]{:S(2)}) collective-permute-start(bf16[128,1920]{1,0:T(8,128)(2,1)} %get-tuple-element.32.refs_0_), channel_id=1, source_target_pairs={{0,16},{8,24},{16,0},{24,8},{1,17},{9,25},{17,1},{25,9},{2,18},{10... | collective-permute-start | bytes 1474568 | tf_op jit(solution)/shard_map/ppermute | solution.py:548
  11.6 1.6 %collective-permute-start = (bf16[128,1920]{1,0:T(8,128)(2,1)}, bf16[128,1920]{1,0:T(8,128)(2,1)}, u32[]{:S(2)}, u32[]{:S(2)}) collective-permute-start(bf16[128,1920]{1,0:T(8,128)(2,1)} %get-tuple-element.32.refs_0_), channel_id=1, source_target_pairs={{0,8},{8,0},{16,24},{24,16},{1,9},{9,1},{17,25},{25,17},{2,10},{10... | collective-permute-start | bytes 1474568 | tf_op jit(solution)/shard_map/ppermute | solution.py:548
  13.2 3.1 %collective-permute-done.1.refs_2_.refs_3_ = bf16[3,896,1792]{2,1,0:T(8,128)(2,1)} collective-permute-done((bf16[3,896,1792]{2,1,0:T(8,128)(2,1)}, bf16[3,896,1792]{2,1,0:T(8,128)(2,1)}, u32[]{:S(2)}, u32[]{:S(2)}) %collective-permute-start.1) | collective-permute-done | bytes 9633824 | tf_op jit(solution)/shard_map/ppermute | solution.py:550
  16.3 9.9 %shard_map.123 = (f32[64,5376]{1,0:T(8,128)}, bf16[64,5376]{1,0:T(8,128)(2,1)}) custom-call(bf16[128,1920]{1,0:T(8,128)(2,1)} %get-tuple-element.32.refs_0_, bf16[3,896,1792]{2,1,0:T(8,128)(2,1)} %bitcast.46, bf16[3,896,1792]{2,1,0:T(8,128)(2,1)} %collective-permute-done.1.refs_2_.refs_3_, bf16[3,16,1792]{2,1,0:T(8,128)(2,1)} %bitcast.50, ...), custom_call_target="tpu_custom_call" | custom-call | flops 199999995904 | bytes 1 | tf_op jit(solution)/shard_map/pallas_call | solution.py:33
  26.3 2.0 %shard_map.124 = (f32[2,64,64]{2,1,0:T(8,128)S(1)}, f32[2,8,64]{2,1,0:T(8,128)S(1)}) custom-call(bf16[64,5376]{1,0:T(8,128)(2,1)} %get-tuple-element.33.refs_0_, s32[8,128]{1,0:T(8,128)S(1)} %bitcast.42, s32[2,64]{1,0:T(2,128)S(1)} %copy-done.11, s32[2,8]{1,0:T(2,128)S(1)} %copy-done.12), custom_call_target="tpu_custom_call" | custom-call | flops 1 | bytes 1 | tf_op jit(solution)/shard_map/pallas_call | solution.py:33
  28.3 5.8 %collective-permute-done.3.refs_2_ = bf16[128,1920]{1,0:T(8,128)(2,1)} collective-permute-done((bf16[128,1920]{1,0:T(8,128)(2,1)}, bf16[128,1920]{1,0:T(8,128)(2,1)}, u32[]{:S(2)}, u32[]{:S(2)}) %collective-permute-start.3) | collective-permute-done | bytes 491552 | tf_op jit(solution)/shard_map/ppermute | solution.py:548
  34.2 1.5 collective-permute-start.6
  35.7 1.5 collective-permute-start.4
  37.2 12.3 %shard_map.126 = (f32[128,5376]{1,0:T(8,128)}, bf16[128,5376]{1,0:T(8,128)(2,1)}) custom-call(bf16[128,1920]{1,0:T(8,128)(2,1)} %collective-permute-done.refs_1_.refs_0_, bf16[128,1920]{1,0:T(8,128)(2,1)} %shard_map.125.refs_1_, bf16[3,896,1792]{2,1,0:T(8,128)(2,1)} %bitcast.47, bf16[3,896,1792]{2,1,0:T(8,128)(2,1)} %collective-permute-done.1.refs_2_.refs_3_, ...), custom_call_target="tpu_custom_call" | custom-call | flops 199999995904 | bytes 1 | tf_op jit(solution)/shard_map/pallas_call | solution.py:33
  50.1 1.4 copy-done.4
  51.5 2.3 %shard_map.127 = (f32[2,16,5376]{2,1,0:T(8,128)S(1)}, bf16[2,16,5376]{2,1,0:T(8,128)(2,1)S(1)}) custom-call(bf16[128,5376]{1,0:T(8,128)(2,1)S(1)} %copy-done.4, f32[2,32,5376]{2,1,0:T(8,128)S(1)} %bitcast.31, bf16[2,32,5376]{2,1,0:T(8,128)(2,1)} %collective-permute-done.4.refs_2_), custom_call_target="tpu_custom_call" | custom-call | flops 1 | bytes 1 | tf_op jit(solution)/shard_map/pallas_call | solution.py:33
  54.5 9.9 %shard_map.128 = (f32[64,5376]{1,0:T(8,128)}, bf16[64,5376]{1,0:T(8,128)(2,1)}) custom-call(bf16[2,16,5376]{2,1,0:T(8,128)(2,1)} %copy-done.13, bf16[128,1920]{1,0:T(8,128)(2,1)} %collective-permute-done.6.refs_1_, bf16[3,896,1792]{2,1,0:T(8,128)(2,1)} %bitcast.48, bf16[3,896,1792]{2,1,0:T(8,128)(2,1)} %collective-permute-done.1.refs_2_.refs_3_, ...), custom_call_target="tpu_custom_call" | custom-call | flops 199999995904 | bytes 1 | tf_op jit(solution)/shard_map/pallas_call | solution.py:33
  64.4 1.6 %collective-permute-start.9 = (bf16[2,32,5376]{2,1,0:T(8,128)(2,1)}, bf16[2,32,5376]{2,1,0:T(8,128)(2,1)S(1)}, u32[]{:S(2)}, u32[]{:S(2)}) collective-permute-start(bf16[2,32,5376]{2,1,0:T(8,128)(2,1)} %bitcast.38), channel_id=1, source_target_pairs={{0,2},{1,5},{2,0},{3,7},{4,6},{5,1},{6,4},{7,3},{8,10},{9,13},{10,... | collective-permute-start | bytes 2064392 | tf_op jit(solution)/shard_map/ppermute | solution.py:573
  66.0 2.2 %collective-permute-done.7.refs_2_ = bf16[4,32,5376]{2,1,0:T(8,128)(2,1)} collective-permute-done((bf16[4,32,5376]{2,1,0:T(8,128)(2,1)}, bf16[4,32,5376]{2,1,0:T(8,128)(2,1)}, u32[]{:S(2)}, u32[]{:S(2)}) %collective-permute-start.7) | collective-permute-done | bytes 1376288 | tf_op jit(solution)/shard_map/ppermute | solution.py:573
  68.2 1.8 %copy-done.1 = f32[128,5376]{1,0:T(8,128)S(1)} copy-done((f32[128,5376]{1,0:T(8,128)S(1)}, f32[128,5376]{1,0:T(8,128)}, u32[]{:S(2)}) %copy-start.1) | copy-done | bytes 2752536
  71.1 2.6 %shard_map.129 = (f32[4,16,5376]{2,1,0:T(8,128)S(1)}, bf16[4,16,5376]{2,1,0:T(8,128)(2,1)S(1)}) custom-call(bf16[64,5376]{1,0:T(8,128)(2,1)S(1)} %copy-done.5, f32[4,32,5376]{2,1,0:T(8,128)S(1)} %bitcast.30, bf16[4,32,5376]{2,1,0:T(8,128)(2,1)} %collective-permute-done.7.refs_2_), custom_call_target="tpu_custom_call" | custom-call | flops 1 | bytes 1 | tf_op jit(solution)/shard_map/pallas_call | solution.py:33
  73.7 1.6 %collective-permute-start.8 = (bf16[4,16,5376]{2,1,0:T(8,128)(2,1)S(1)}, bf16[4,16,5376]{2,1,0:T(8,128)(2,1)S(1)}, u32[]{:S(2)}, u32[]{:S(2)}) collective-permute-start(bf16[4,16,5376]{2,1,0:T(8,128)(2,1)S(1)} %get-tuple-element.42.refs_0_), channel_id=1, source_target_pairs={{0,4},{1,3},{2,6},{3,1},{4,0},{5,7},{6,2},{7,5},{8,12},{9,11},{10,... | collective-permute-start | bytes 2064392 | tf_op jit(solution)/shard_map/ppermute | solution.py:573
  75.8 1.2 collective-permute-done.9.refs_2_
  77.4 2.6 %collective-permute-start.10 = (bf16[2,16,5376]{2,1,0:T(8,128)(2,1)S(1)}, bf16[2,16,5376]{2,1,0:T(8,128)(2,1)S(1)}, u32[]{:S(2)}, u32[]{:S(2)}) collective-permute-start(bf16[2,16,5376]{2,1,0:T(8,128)(2,1)S(1)} %get-tuple-element.45), channel_id=1, source_target_pairs={{0,4},{1,3},{2,6},{3,1},{4,0},{5,7},{6,2},{7,5},{8,12},{9,11},{10,... | collective-permute-start | bytes 1032200 | tf_op jit(solution)/shard_map/ppermute | solution.py:573
  80.0 8.3 %collective-permute-done.5 = bf16[2,16,5376]{2,1,0:T(8,128)(2,1)S(1)} collective-permute-done((bf16[2,16,5376]{2,1,0:T(8,128)(2,1)S(1)}, bf16[2,16,5376]{2,1,0:T(8,128)(2,1)S(1)}, u32[]{:S(2)}, u32[]{:S(2)}) %collective-permute-start.5) | collective-permute-done | bytes 344096 | tf_op jit(solution)/shard_map/ppermute | solution.py:573
  88.4 3.7 %collective-permute-done.10 = bf16[2,16,5376]{2,1,0:T(8,128)(2,1)S(1)} collective-permute-done((bf16[2,16,5376]{2,1,0:T(8,128)(2,1)S(1)}, bf16[2,16,5376]{2,1,0:T(8,128)(2,1)S(1)}, u32[]{:S(2)}, u32[]{:S(2)}) %collective-permute-start.10) | collective-permute-done | bytes 344096 | tf_op jit(solution)/shard_map/ppermute | solution.py:573
  92.7 10.9 %shard_map.132 = (bf16[64,1792]{1,0:T(8,128)(2,1)S(1)}, bf16[2,8,1792]{2,1,0:T(8,128)(2,1)S(1)}) custom-call(s32[2]{0:T(128)S(1)} %copy-done.10, bf16[64,5376]{1,0:T(8,128)(2,1)S(1)} %shard_map.131.refs_1_, f32[2,64,64]{2,1,0:T(8,128)S(1)} %get-tuple-element.46.refs_2_, f32[2,8,64]{2,1,0:T(8,128)S(1)} %copy-done.8, bf16[2,2,2048,1792]{3,2,1,0:T(8,128)(2,1)} %refs_4_.3), custom_call_target="tpu_custom_call" | custom-call | flops 1 | bytes 1 | tf_op jit(solution)/shard_map/pallas_call | solution.py:33
  104.7 2.5 %collective-permute-start.11 = (bf16[64,1792]{1,0:T(8,128)(2,1)S(1)}, bf16[64,1792]{1,0:T(8,128)(2,1)S(1)}, u32[]{:S(2)}, u32[]{:S(2)}) collective-permute-start(bf16[64,1792]{1,0:T(8,128)(2,1)S(1)} %get-tuple-element.47.refs_0_.refs_1_), channel_id=1, source_target_pairs={{0,4},{1,3},{2,6},{3,1},{4,0},{5,7},{6,2},{7,5},{8,12},{9,11},{10,... | collective-permute-start | bytes 688136 | tf_op jit(solution)/shard_map/ppermute | solution.py:611
  107.6 9.2 %shard_map.134 = (bf16[64,1792]{1,0:T(8,128)(2,1)S(1)}, bf16[2,8,1792]{2,1,0:T(8,128)(2,1)S(1)}) custom-call(s32[2]{0:T(128)S(1)} %copy-done.10, bf16[64,5376]{1,0:T(8,128)(2,1)S(1)} %shard_map.133.refs_1_, f32[2,64,64]{2,1,0:T(8,128)S(1)} %get-tuple-element.46.refs_2_, f32[2,8,64]{2,1,0:T(8,128)S(1)} %copy-done.8, bf16[2,2,2048,1792]{3,2,1,0:T(8,128)(2,1)} %refs_4_.3), custom_call_target="tpu_custom_call" | custom-call | flops 1 | bytes 1 | tf_op jit(solution)/shard_map/pallas_call | solution.py:33
  117.1 3.4 %collective-permute-start.16 = (bf16[64,1792]{1,0:T(8,128)(2,1)S(1)}, bf16[64,1792]{1,0:T(8,128)(2,1)S(1)}, u32[]{:S(2)}, u32[]{:S(2)}) collective-permute-start(bf16[64,1792]{1,0:T(8,128)(2,1)S(1)} %get-tuple-element.48.refs_0_.refs_1_), channel_id=1, source_target_pairs={{0,2},{1,5},{2,0},{3,7},{4,6},{5,1},{6,4},{7,3},{8,10},{9,13},{10,... | collective-permute-start | bytes 688136 | tf_op jit(solution)/shard_map/ppermute | solution.py:610
  122.2 4.2 %collective-permute-done.17.refs_4_ = bf16[64,1792]{1,0:T(8,128)(2,1)S(1)} collective-permute-done((bf16[64,1792]{1,0:T(8,128)(2,1)S(1)}, bf16[64,1792]{1,0:T(8,128)(2,1)S(1)}, u32[]{:S(2)}, u32[]{:S(2)}) %collective-permute-start.17) | collective-permute-done | bytes 229408 | tf_op jit(solution)/shard_map/ppermute | solution.py:612
  126.4 5.0 %collective-permute-done.16.refs_3_ = bf16[64,1792]{1,0:T(8,128)(2,1)S(1)} collective-permute-done((bf16[64,1792]{1,0:T(8,128)(2,1)S(1)}, bf16[64,1792]{1,0:T(8,128)(2,1)S(1)}, u32[]{:S(2)}, u32[]{:S(2)}) %collective-permute-start.16) | collective-permute-done | bytes 229408 | tf_op jit(solution)/shard_map/ppermute | solution.py:610
  131.6 2.5 %collective-permute-done.20.refs_1_ = bf16[256,1792]{1,0:T(8,128)(2,1)S(1)} collective-permute-done((bf16[256,1792]{1,0:T(8,128)(2,1)S(1)}, bf16[256,1792]{1,0:T(8,128)(2,1)S(1)}, u32[]{:S(2)}, u32[]{:S(2)}) %collective-permute-start.20) | collective-permute-done | bytes 917536 | tf_op jit(solution)/shard_map/ppermute | solution.py:621
  135.7 1.8 %collective-permute-start.19 = (bf16[448,128]{1,0:T(8,128)(2,1)S(1)}, bf16[448,128]{1,0:T(8,128)(2,1)S(1)}, u32[]{:S(2)}, u32[]{:S(2)}) collective-permute-start(bf16[448,128]{1,0:T(8,128)(2,1)S(1)} %get-tuple-element.52), channel_id=1, source_target_pairs={{0,16},{8,24},{16,0},{24,8},{1,17},{9,25},{17,1},{25,9},{2,18},{10... | collective-permute-start | bytes 344072 | tf_op jit(solution)/shard_map/ppermute | solution.py:548
  137.6 7.7 %collective-permute-done.21.refs_1_ = bf16[2,448,128]{2,1,0:T(8,128)(2,1)S(1)} collective-permute-done((bf16[2,448,128]{2,1,0:T(8,128)(2,1)S(1)}, bf16[2,448,128]{2,1,0:T(8,128)(2,1)S(1)}, u32[]{:S(2)}, u32[]{:S(2)}) %collective-permute-start.21) | collective-permute-done | bytes 229408 | tf_op jit(solution)/shard_map/ppermute | solution.py:548
  146.7 6.0 %collective-permute-done.22.refs_4_ = bf16[448,128]{1,0:T(8,128)(2,1)S(1)} collective-permute-done((bf16[448,128]{1,0:T(8,128)(2,1)S(1)}, bf16[448,128]{1,0:T(8,128)(2,1)S(1)}, u32[]{:S(2)}, u32[]{:S(2)}) %collective-permute-start.22) | collective-permute-done | bytes 114720 | tf_op jit(solution)/shard_map/ppermute | solution.py:548
  (68 shorter events, 12.5 us)
Async XLA Ops:
  0.6 15.7 %collective-permute-start.1 = (bf16[3,896,1792]{2,1,0:T(8,128)(2,1)}, bf16[3,896,1792]{2,1,0:T(8,128)(2,1)}, u32[]{:S(2)}, u32[]{:S(2)}) collective-permute-start(bf16[3,896,1792]{2,1,0:T(8,128)(2,1)} %bitcast.45), channel_id=1, source_target_pairs={{0,1},{1,0},{2,3},{3,2},{4,5},{5,4},{6,7},{7,6},{8,9},{9,8},{10,11... | collective-permute-start | bytes 28901384 | tf_op jit(solution)/shard_map/ppermute | solution.py:550
  1.1 12.1 %collective-permute-start.2 = (bf16[3,16,1792]{2,1,0:T(8,128)(2,1)}, bf16[3,16,1792]{2,1,0:T(8,128)(2,1)S(1)}, u32[]{:S(2)}, u32[]{:S(2)}) collective-permute-start(bf16[3,16,1792]{2,1,0:T(8,128)(2,1)} %bitcast.49), channel_id=1, source_target_pairs={{0,1},{1,0},{2,3},{3,2},{4,5},{5,4},{6,7},{7,6},{8,9},{9,8},{10,11... | collective-permute-start | bytes 516104 | tf_op jit(solution)/shard_map/ppermute | solution.py:551
  7.6 26.5 %collective-permute-start.3 = (bf16[128,1920]{1,0:T(8,128)(2,1)}, bf16[128,1920]{1,0:T(8,128)(2,1)}, u32[]{:S(2)}, u32[]{:S(2)}) collective-permute-start(bf16[128,1920]{1,0:T(8,128)(2,1)} %get-tuple-element.32.refs_0_), channel_id=1, source_target_pairs={{0,16},{8,24},{16,0},{24,8},{1,17},{9,25},{17,1},{25,9},{2,18},{10... | collective-permute-start | bytes 1474568 | tf_op jit(solution)/shard_map/ppermute | solution.py:548
  11.6 22.6 %collective-permute-start = (bf16[128,1920]{1,0:T(8,128)(2,1)}, bf16[128,1920]{1,0:T(8,128)(2,1)}, u32[]{:S(2)}, u32[]{:S(2)}) collective-permute-start(bf16[128,1920]{1,0:T(8,128)(2,1)} %get-tuple-element.32.refs_0_), channel_id=1, source_target_pairs={{0,8},{8,0},{16,24},{24,16},{1,9},{9,1},{17,25},{25,17},{2,10},{10... | collective-permute-start | bytes 1474568 | tf_op jit(solution)/shard_map/ppermute | solution.py:548
  16.3 9.9 %copy-start.9 = (s32[1024]{0:T(1024)S(1)}, s32[1024]{0:T(1024)}, u32[]{:S(2)}) copy-start(s32[1024]{0:T(1024)} %param.12) | copy-start | bytes 12292
  16.3 9.9 %copy-start.11 = (s32[2,64]{1,0:T(2,128)S(1)}, s32[2,64]{1,0:T(2,128)}, u32[]{:S(2)}) copy-start(s32[2,64]{1,0:T(2,128)} %refs_2_.1) | copy-start | bytes 1540
  16.3 9.9 %copy-start.12 = (s32[2,8]{1,0:T(2,128)S(1)}, s32[2,8]{1,0:T(2,128)}, u32[]{:S(2)}) copy-start(s32[2,8]{1,0:T(2,128)} %refs_3_.3) | copy-start | bytes 196
  28.2 7.5 %copy-start.7 = (f32[2,8,64]{2,1,0:T(8,128)}, f32[2,8,64]{2,1,0:T(8,128)S(1)}, u32[]{:S(2)}) copy-start(f32[2,8,64]{2,1,0:T(8,128)S(1)} %get-tuple-element.34.refs_0_.refs_3_) | copy-start | bytes 12292
  34.2 20.3 %collective-permute-start.6 = (bf16[128,1920]{1,0:T(8,128)(2,1)}, bf16[128,1920]{1,0:T(8,128)(2,1)}, u32[]{:S(2)}, u32[]{:S(2)}) collective-permute-start(bf16[128,1920]{1,0:T(8,128)(2,1)} %shard_map.125.refs_1_), channel_id=1, source_target_pairs={{0,8},{8,0},{16,24},{24,16},{1,9},{9,1},{17,25},{25,17},{2,10},{10... | collective-permute-start | bytes 1474568 | tf_op jit(solution)/shard_map/ppermute | solution.py:548
  35.7 14.4 %collective-permute-start.4 = (bf16[2,32,5376]{2,1,0:T(8,128)(2,1)}, bf16[2,32,5376]{2,1,0:T(8,128)(2,1)}, u32[]{:S(2)}, u32[]{:S(2)}) collective-permute-start(bf16[2,32,5376]{2,1,0:T(8,128)(2,1)} %bitcast.5), channel_id=1, source_target_pairs={{0,2},{1,5},{2,0},{3,7},{4,6},{5,1},{6,4},{7,3},{8,10},{9,13},{10,... | collective-permute-start | bytes 2064392 | tf_op jit(solution)/shard_map/ppermute | solution.py:573
  37.2 12.9 %copy-start.2 = (f32[64,5376]{1,0:T(8,128)S(1)}, f32[64,5376]{1,0:T(8,128)}, u32[]{:S(2)}) copy-start(f32[64,5376]{1,0:T(8,128)} %get-tuple-element.36) | copy-start | bytes 4128772
  49.5 18.7 %collective-permute-start.7 = (bf16[4,32,5376]{2,1,0:T(8,128)(2,1)}, bf16[4,32,5376]{2,1,0:T(8,128)(2,1)}, u32[]{:S(2)}, u32[]{:S(2)}) collective-permute-start(bf16[4,32,5376]{2,1,0:T(8,128)(2,1)} %bitcast.33), channel_id=1, source_target_pairs={{0,2},{1,5},{2,0},{3,7},{4,6},{5,1},{6,4},{7,3},{8,10},{9,13},{10,... | collective-permute-start | bytes 4128776 | tf_op jit(solution)/shard_map/ppermute | solution.py:573
  64.4 12.6 %collective-permute-start.9 = (bf16[2,32,5376]{2,1,0:T(8,128)(2,1)}, bf16[2,32,5376]{2,1,0:T(8,128)(2,1)S(1)}, u32[]{:S(2)}, u32[]{:S(2)}) collective-permute-start(bf16[2,32,5376]{2,1,0:T(8,128)(2,1)} %bitcast.38), channel_id=1, source_target_pairs={{0,2},{1,5},{2,0},{3,7},{4,6},{5,1},{6,4},{7,3},{8,10},{9,13},{10,... | collective-permute-start | bytes 2064392 | tf_op jit(solution)/shard_map/ppermute | solution.py:573
  71.1 4.2 %copy-start.14 = (bf16[2,16,5376]{2,1,0:T(8,128)(2,1)S(1)}, bf16[2,16,5376]{2,1,0:T(8,128)(2,1)}, u32[]{:S(2)}) copy-start(bf16[2,16,5376]{2,1,0:T(8,128)(2,1)} %copy-done.13) | copy-start | bytes 1032196
  71.1 5.9 %copy-start.3 = (f32[64,5376]{1,0:T(8,128)S(1)}, f32[64,5376]{1,0:T(8,128)}, u32[]{:S(2)}) copy-start(f32[64,5376]{1,0:T(8,128)} %get-tuple-element.43) | copy-start | bytes 4128772
  73.7 18.4 %collective-permute-start.8 = (bf16[4,16,5376]{2,1,0:T(8,128)(2,1)S(1)}, bf16[4,16,5376]{2,1,0:T(8,128)(2,1)S(1)}, u32[]{:S(2)}, u32[]{:S(2)}) collective-permute-start(bf16[4,16,5376]{2,1,0:T(8,128)(2,1)S(1)} %get-tuple-element.42.refs_0_), channel_id=1, source_target_pairs={{0,4},{1,3},{2,6},{3,1},{4,0},{5,7},{6,2},{7,5},{8,12},{9,11},{10,... | collective-permute-start | bytes 2064392 | tf_op jit(solution)/shard_map/ppermute | solution.py:573
  75.2 13.1 %collective-permute-start.5 = (bf16[2,16,5376]{2,1,0:T(8,128)(2,1)S(1)}, bf16[2,16,5376]{2,1,0:T(8,128)(2,1)S(1)}, u32[]{:S(2)}, u32[]{:S(2)}) collective-permute-start(bf16[2,16,5376]{2,1,0:T(8,128)(2,1)S(1)} %copy-done.14), channel_id=1, source_target_pairs={{0,4},{1,3},{2,6},{3,1},{4,0},{5,7},{6,2},{7,5},{8,12},{9,11},{10,... | collective-permute-start | bytes 1032200 | tf_op jit(solution)/shard_map/ppermute | solution.py:573
  77.4 14.6 %collective-permute-start.10 = (bf16[2,16,5376]{2,1,0:T(8,128)(2,1)S(1)}, bf16[2,16,5376]{2,1,0:T(8,128)(2,1)S(1)}, u32[]{:S(2)}, u32[]{:S(2)}) collective-permute-start(bf16[2,16,5376]{2,1,0:T(8,128)(2,1)S(1)} %get-tuple-element.45), channel_id=1, source_target_pairs={{0,4},{1,3},{2,6},{3,1},{4,0},{5,7},{6,2},{7,5},{8,12},{9,11},{10,... | collective-permute-start | bytes 1032200 | tf_op jit(solution)/shard_map/ppermute | solution.py:573
  103.6 13.2 %collective-permute-start.13 = (bf16[64,1792]{1,0:T(8,128)(2,1)S(1)}, bf16[64,1792]{1,0:T(8,128)(2,1)S(1)}, u32[]{:S(2)}, u32[]{:S(2)}) collective-permute-start(bf16[64,1792]{1,0:T(8,128)(2,1)S(1)} %get-tuple-element.47.refs_0_.refs_1_), channel_id=1, source_target_pairs={{0,6},{1,7},{2,4},{3,5},{4,2},{5,3},{6,0},{7,1},{8,14},{9,15},{10,... | collective-permute-start | bytes 688136 | tf_op jit(solution)/shard_map/ppermute | solution.py:612
  103.7 13.1 %collective-permute-start.12 = (bf16[64,1792]{1,0:T(8,128)(2,1)S(1)}, bf16[64,1792]{1,0:T(8,128)(2,1)S(1)}, u32[]{:S(2)}, u32[]{:S(2)}) collective-permute-start(bf16[64,1792]{1,0:T(8,128)(2,1)S(1)} %get-tuple-element.47.refs_0_.refs_1_), channel_id=1, source_target_pairs={{0,2},{1,5},{2,0},{3,7},{4,6},{5,1},{6,4},{7,3},{8,10},{9,13},{10,... | collective-permute-start | bytes 688136 | tf_op jit(solution)/shard_map/ppermute | solution.py:610
  104.7 12.2 %collective-permute-start.11 = (bf16[64,1792]{1,0:T(8,128)(2,1)S(1)}, bf16[64,1792]{1,0:T(8,128)(2,1)S(1)}, u32[]{:S(2)}, u32[]{:S(2)}) collective-permute-start(bf16[64,1792]{1,0:T(8,128)(2,1)S(1)} %get-tuple-element.47.refs_0_.refs_1_), channel_id=1, source_target_pairs={{0,4},{1,3},{2,6},{3,1},{4,0},{5,7},{6,2},{7,5},{8,12},{9,11},{10,... | collective-permute-start | bytes 688136 | tf_op jit(solution)/shard_map/ppermute | solution.py:611
  116.8 3.8 %copy-start = (bf16[1792,448]{0,1:T(8,128)(2,1)S(1)}, bf16[1792,448]{0,1:T(8,128)(2,1)}, u32[]{:S(2)}) copy-start(bf16[1792,448]{0,1:T(8,128)(2,1)} %param.21) | copy-start | bytes 4816900
  116.9 3.6 %collective-permute-start.14 = (bf16[256,1792]{1,0:T(8,128)(2,1)S(1)}, bf16[256,1792]{1,0:T(8,128)(2,1)S(1)}, u32[]{:S(2)}, u32[]{:S(2)}) collective-permute-start(bf16[256,1792]{1,0:T(8,128)(2,1)S(1)} %shard_map.135.refs_0_), channel_id=1, source_target_pairs={{0,1},{1,0},{2,3},{3,2},{4,5},{5,4},{6,7},{7,6},{8,9},{9,8},{10,11... | collective-permute-start | bytes 2752520 | tf_op jit(solution)/shard_map/ppermute | solution.py:621
  117.0 9.4 %collective-permute-start.17 = (bf16[64,1792]{1,0:T(8,128)(2,1)S(1)}, bf16[64,1792]{1,0:T(8,128)(2,1)S(1)}, u32[]{:S(2)}, u32[]{:S(2)}) collective-permute-start(bf16[64,1792]{1,0:T(8,128)(2,1)S(1)} %get-tuple-element.48.refs_0_.refs_1_), channel_id=1, source_target_pairs={{0,6},{1,7},{2,4},{3,5},{4,2},{5,3},{6,0},{7,1},{8,14},{9,15},{10,... | collective-permute-start | bytes 688136 | tf_op jit(solution)/shard_map/ppermute | solution.py:612
  117.1 14.3 %collective-permute-start.16 = (bf16[64,1792]{1,0:T(8,128)(2,1)S(1)}, bf16[64,1792]{1,0:T(8,128)(2,1)S(1)}, u32[]{:S(2)}, u32[]{:S(2)}) collective-permute-start(bf16[64,1792]{1,0:T(8,128)(2,1)S(1)} %get-tuple-element.48.refs_0_.refs_1_), channel_id=1, source_target_pairs={{0,2},{1,5},{2,0},{3,7},{4,6},{5,1},{6,4},{7,3},{8,10},{9,13},{10,... | collective-permute-start | bytes 688136 | tf_op jit(solution)/shard_map/ppermute | solution.py:610
  120.5 10.9 %collective-permute-start.15 = (bf16[64,1792]{1,0:T(8,128)(2,1)S(1)}, bf16[64,1792]{1,0:T(8,128)(2,1)S(1)}, u32[]{:S(2)}, u32[]{:S(2)}) collective-permute-start(bf16[64,1792]{1,0:T(8,128)(2,1)S(1)} %get-tuple-element.48.refs_0_.refs_1_), channel_id=1, source_target_pairs={{0,4},{1,3},{2,6},{3,1},{4,0},{5,7},{6,2},{7,5},{8,12},{9,11},{10,... | collective-permute-start | bytes 688136 | tf_op jit(solution)/shard_map/ppermute | solution.py:611
  121.6 9.9 %collective-permute-start.18 = (bf16[2,448,128]{2,1,0:T(8,128)(2,1)S(1)}, bf16[2,448,128]{2,1,0:T(8,128)(2,1)S(1)}, u32[]{:S(2)}, u32[]{:S(2)}) collective-permute-start(bf16[2,448,128]{2,1,0:T(8,128)(2,1)S(1)} %get-tuple-element.50), channel_id=1, source_target_pairs={{0,8},{8,0},{16,24},{24,16},{1,9},{9,1},{17,25},{25,17},{2,10},{10... | collective-permute-start | bytes 688136 | tf_op jit(solution)/shard_map/ppermute | solution.py:548
  131.5 21.2 %copy-start.6 = (bf16[256,256]{1,0:T(8,128)(2,1)S(1)}, bf16[256,256]{1,0:T(8,128)(2,1)}, u32[]{:S(2)}) copy-start(bf16[256,256]{1,0:T(8,128)(2,1)} %get-tuple-element.31.refs_0_) | copy-start | bytes 393220
  131.5 2.5 %collective-permute-start.20 = (bf16[256,1792]{1,0:T(8,128)(2,1)S(1)}, bf16[256,1792]{1,0:T(8,128)(2,1)S(1)}, u32[]{:S(2)}, u32[]{:S(2)}) collective-permute-start(bf16[256,1792]{1,0:T(8,128)(2,1)S(1)} %get-tuple-element.53.refs_0_), channel_id=1, source_target_pairs={{0,1},{1,0},{2,3},{3,2},{4,5},{5,4},{6,7},{7,6},{8,9},{9,8},{10,11... | collective-permute-start | bytes 2752520 | tf_op jit(solution)/shard_map/ppermute | solution.py:621
  135.1 10.2 %collective-permute-start.21 = (bf16[2,448,128]{2,1,0:T(8,128)(2,1)S(1)}, bf16[2,448,128]{2,1,0:T(8,128)(2,1)S(1)}, u32[]{:S(2)}, u32[]{:S(2)}) collective-permute-start(bf16[2,448,128]{2,1,0:T(8,128)(2,1)S(1)} %get-tuple-element.55), channel_id=1, source_target_pairs={{0,8},{8,0},{16,24},{24,16},{1,9},{9,1},{17,25},{25,17},{2,10},{10... | collective-permute-start | bytes 688136 | tf_op jit(solution)/shard_map/ppermute | solution.py:548
  135.7 11.0 %collective-permute-start.19 = (bf16[448,128]{1,0:T(8,128)(2,1)S(1)}, bf16[448,128]{1,0:T(8,128)(2,1)S(1)}, u32[]{:S(2)}, u32[]{:S(2)}) collective-permute-start(bf16[448,128]{1,0:T(8,128)(2,1)S(1)} %get-tuple-element.52), channel_id=1, source_target_pairs={{0,16},{8,24},{16,0},{24,8},{1,17},{9,25},{17,1},{25,9},{2,18},{10... | collective-permute-start | bytes 344072 | tf_op jit(solution)/shard_map/ppermute | solution.py:548
  145.3 7.4 %collective-permute-start.22 = (bf16[448,128]{1,0:T(8,128)(2,1)S(1)}, bf16[448,128]{1,0:T(8,128)(2,1)S(1)}, u32[]{:S(2)}, u32[]{:S(2)}) collective-permute-start(bf16[448,128]{1,0:T(8,128)(2,1)S(1)} %get-tuple-element.57), channel_id=1, source_target_pairs={{0,16},{8,24},{16,0},{24,8},{1,17},{9,25},{17,1},{25,9},{2,18},{10... | collective-permute-start | bytes 344072 | tf_op jit(solution)/shard_map/ppermute | solution.py:548
  (7 other events, 9.5 us)
